TPU v7x, 256 devices: a whole 4x4x8 slice. The times are simulated.
256 devices in a mesh: sample: 16 (over z, core), feature: 16 (over y, x).
Axes of the slice: x: 4, y: 4, z: 8, core: 2. Of those that a mesh axis runs over, the one named last changes fastest.
Arguments:
- slab: bfloat16 [49152, 16384], P('sample', 'feature'), may hold values from -20 to 20
- omega: int32 [16384, 512], P('feature'), may hold values from -8 to 8
Outputs:
- coeffs: float32 [512, 16384], P('sample', 'feature')
- factor: float32 [512, 512], replicated
All inputs are finite; a program needn't handle non-finite values.
Results may differ from a plain program's by a relative error of at most 0.0019.
Values may be sent and summed in bfloat16 or wider, within the bound.
A program may use at most 128 MiB of HBM per device.

v0:
```python
import math

import jax
import jax.numpy as jnp
from jax import lax
from jax.sharding import PartitionSpec as P

D = 16384


def shards(slab, omega):
    omega_b = omega.astype(jnp.bfloat16)
    scale = 1.0 / math.sqrt(24.0 * D)
    tokens_all = slab.shape[0] * lax.axis_size("sample")
    partial_sketch = jnp.dot(slab, omega_b, preferred_element_type=jnp.float32)
    sketch = lax.psum(partial_sketch, "feature") * scale
    local_gram = jnp.dot(
        sketch.T, sketch, preferred_element_type=jnp.float32, precision=lax.Precision.HIGHEST
    )
    gram = lax.psum(local_gram, "sample")
    lower = jnp.linalg.cholesky(gram)
    basis_t = lax.linalg.triangular_solve(lower, sketch.T, left_side=True, lower=True).astype(
        jnp.bfloat16
    )
    coeffs = lax.psum_scatter(
        jnp.dot(basis_t, slab, preferred_element_type=jnp.float32),
        "sample",
        scatter_dimension=0,
        tiled=True,
    )
    factor = lower.T / math.sqrt(tokens_all)
    return (coeffs, factor)


def solution(mesh):
    placed = (P("sample", "feature"), P("feature", None))
    return jax.shard_map(
        shards, mesh=mesh, in_specs=placed, out_specs=(P("sample", "feature"), P()), check_vma=False
    )
```

profile of v0, /device:TPU:2, one launch (start us, length us, event | category | flops | bytes accessed | tf_op | source)
XLA Modules:
  0.0 508.5 jit_solution(8240688568270891553)
XLA Ops:
  7.2 9.5 %fusion.26 = f32[3072,512]{1,0:T(8,128)} fusion(bf16[3072,1024]{1,0:T(8,128)(2,1)} %param.2, s32[1024,512]{1,0:T(8,128)} %param.3), kind=kOutput, calls=%fused_computation.38 | convolution fusion | flops 3221749760 | bytes 14680064 | tf_op jit(solution)/shard_map/dot_general | solution.py:15
  16.8 135.4 %all-reduce.4.cloned.1.call-done = f32[3072,512]{1,0:T(8,128)} async-done(((f32[3072,512]{1,0:T(8,128)}), f32[3072,512]{1,0:T(8,128)}) %all-reduce.4.cloned.1.call-update) | async-done | bytes 6291472 | tf_op jit(solution)/shard_map/psum | solution.py:16
  152.2 15.2 %fusion = f32[512,512]{0,1:T(8,128)} fusion(f32[3072,512]{1,0:T(8,128)} %all-reduce.4.cloned.1.call-done), kind=kOutput, calls=%fused_computation.3 | convolution fusion | flops 9665249280 | bytes 7340032 | tf_op jit(solution)/shard_map/dot_general | solution.py:17
  167.7 6.2 %multiply_bitcast_fusion = f32[512,3072]{0,1:T(8,128)} fusion(f32[3072,512]{1,0:T(8,128)} %all-reduce.4.cloned.1.call-done), kind=kLoop, calls=%fused_computation.2 | loop fusion | flops 1572864 | bytes 12582912 | tf_op jit(solution)/shard_map/transpose | solution.py:18
  173.9 105.1 %all-reduce.6.cloned.1.call-done = f32[512,512]{0,1:T(8,128)} async-done(((f32[512,512]{0,1:T(8,128)}), f32[512,512]{0,1:T(8,128)}) %all-reduce.6.cloned.1.call-update) | async-done | bytes 1048592 | tf_op jit(solution)/shard_map/psum | solution.py:20
  279.0 1.6 copy.5
  280.9 11.7 %cholesky.104 = f32[128,128]{1,0:T(8,128)S(1)} custom-call(f32[128,128]{1,0:T(8,128)S(1)} %cholesky.266), custom_call_target="Cholesky" | custom-call | tf_op jit(solution)/shard_map/jit(cholesky)/cholesky | solution.py:21
  292.7 9.8 %custom-call.30 = f32[1,128,128]{1,2,0:T(8,128)S(1)} custom-call(f32[1,128,128]{2,1,0:T(8,128)S(1)} %get-tuple-element.33), custom_call_target="InvertDiagBlocksLowerTriangular" | custom-call | tf_op jit(solution)/shard_map/jit(cholesky)/cholesky | solution.py:21
  303.3 11.7 %cholesky.217 = f32[128,128]{1,0:T(8,128)S(1)} custom-call(f32[128,128]{1,0:T(8,128)S(1)} %cholesky.270), custom_call_target="Cholesky" | custom-call | tf_op jit(solution)/shard_map/jit(cholesky)/cholesky | solution.py:21
  315.0 10.2 %custom-call.31 = f32[1,128,128]{1,2,0:T(8,128)S(1)} custom-call(f32[1,128,128]{2,1,0:T(8,128)S(1)} %get-tuple-element.30), custom_call_target="InvertDiagBlocksLowerTriangular" | custom-call | tf_op jit(solution)/shard_map/jit(cholesky)/cholesky | solution.py:21
  325.9 11.7 %cholesky.238 = f32[128,128]{1,0:T(8,128)S(1)} custom-call(f32[128,128]{1,0:T(8,128)S(1)} %cholesky.275), custom_call_target="Cholesky" | custom-call | tf_op jit(solution)/shard_map/jit(cholesky)/cholesky | solution.py:21
  338.3 9.8 %custom-call.32 = f32[1,128,128]{1,2,0:T(8,128)S(1)} custom-call(f32[1,128,128]{2,1,0:T(8,128)S(1)} %get-tuple-element.27), custom_call_target="InvertDiagBlocksLowerTriangular" | custom-call | tf_op jit(solution)/shard_map/jit(cholesky)/cholesky | solution.py:21
  348.7 11.9 %cholesky.255 = f32[128,128]{1,0:T(8,128)S(1)} custom-call(f32[128,128]{1,0:T(8,128)S(1)} %convolution_subtract_fusion.4), custom_call_target="Cholesky" | custom-call | tf_op jit(solution)/shard_map/jit(cholesky)/cholesky | solution.py:21
  364.7 7.7 %while.1 = (s32[]{:T(128)}, f32[512,512]{1,0:T(8,128)S(1)}, s32[4,2]{0,1:T(2,128)S(1)}, f32[4,128,128]{2,1,0:T(8,128)S(1)}, s32[]{:T(128)}) while((s32[]{:T(128)}, f32[512,512]{1,0:T(8,128)S(1)}, s32[4,2]{0,1:T(2,128)S(1)}, f32[4,128,128]{2,1,0:T(8,128)S(1)}, s32[]{:T(128)}) %tuple.36), condition=%wide.while_cond, body=%wide.while_body.sunk | while | flops 2 | bytes 131189 | solution.py:22
  372.5 39.3 %custom-call.33 = f32[4,128,128]{1,2,0:T(8,128)S(1)} custom-call(f32[4,128,128]{2,1,0:T(8,128)S(1)} %get-tuple-element.9), custom_call_target="InvertDiagBlocksLowerTriangular" | custom-call | tf_op jit(solution)/shard_map/triangular_solve | solution.py:22
  411.8 3.1 fusion.52
  414.9 4.2 convolution_subtract_fusion
  419.1 1.5 fusion.51
  420.7 5.4 %convolution_subtract_fusion.1 = f32[128,3072]{0,1:T(8,128)S(1)} fusion(f32[128,3072]{1,0:T(8,128)S(1)} %get-tuple-element.39, f32[128,3072]{1,0:T(8,128)S(1)} %get-tuple-element.41, f32[512,3072]{0,1:T(8,128)S(1)} %bitcast.61, f32[512,512]{1,0:T(8,128)S(1)} %get-tuple-element.95), kind=kOutput, calls=%fused_computation.12 | convolution fusion | flops 1209139200 | bytes 6422528 | tf_op jit(solution)/shard_map/triangular_solve | solution.py:22
  426.1 1.8 fusion.50
  427.8 8.0 %fusion.8 = f32[128,3072]{0,1:T(8,128)S(1)} fusion(f32[128,3072]{1,0:T(8,128)S(1)} %get-tuple-element.37, f32[128,3072]{1,0:T(8,128)S(1)} %get-tuple-element.39, f32[128,3072]{1,0:T(8,128)S(1)} %get-tuple-element.41, f32[512,3072]{0,1:T(8,128)S(1)} %bitcast.61, f32[512,512]{1,0:T(8,128)S(1)} %get-tuple-element.95), kind=kOutput, calls=%fused_computation.13 | convolution fusion | flops 1814691840 | bytes 8060928 | tf_op jit(solution)/shard_map/triangular_solve | solution.py:22
  435.8 1.5 convolution_convert_fusion
  437.4 4.8 fusion.14
  443.6 58.2 %reduce-scatter.2.cloned.1.call-done = f32[32,1024]{1,0:T(8,128)} async-done(((f32[512,1024]{1,0:T(8,128)}), f32[32,1024]{1,0:T(8,128)}) %reduce-scatter.2.cloned.1.call-update) | async-done | bytes 131088 | tf_op jit(solution)/shard_map/reduce_scatter | solution.py:25
  (53 shorter events, 14.0 us)
Async XLA Ops:
  7.2 145.1 %all-reduce.4.cloned.1.call-start = ((), (), s32[]{:S(2)}) async-start(), calls=%async_computation.1 | async-start | bytes 12582912 | tf_op jit(solution)/shard_map/psum | solution.py:16
  16.8 262.3 %all-reduce.6.cloned.1.call-start = ((), (), s32[]{:S(2)}) async-start(), calls=%async_computation.2 | async-start | bytes 2097152 | tf_op jit(solution)/shard_map/psum | solution.py:20
  167.5 334.3 %reduce-scatter.2.cloned.1.call-start = ((), (), s32[]{:S(2)}) async-start(), calls=%async_computation.3 | async-start | bytes 2228224 | tf_op jit(solution)/shard_map/reduce_scatter | solution.py:25
  279.0 1.7 copy-start
  411.8 8.8 %slice-start = ((s8[6291456]{0:T(1024)(128)(4,1)}), s8[4194304]{0:T(1024)(128)(4,1)S(1)}, s32[]{:S(2)}) async-start(s8[6291456]{0:T(1024)(128)(4,1)} %bitcast.60), calls=%async_computation.4 | async-start | bytes 8388608
  414.9 5.8 %slice-start.1 = ((s8[6291456]{0:T(1024)(128)(4,1)}), s8[2097152]{0:T(1024)(128)(4,1)S(1)}, s32[]{:S(2)}) async-start(s8[6291456]{0:T(1024)(128)(4,1)} %bitcast.60), calls=%async_computation.5 | async-start | bytes 4194304
  426.1 11.3 %slice-start.2 = ((s8[6291456]{0:T(1024)(128)(4,1)}), s8[4194304]{0:T(1024)(128)(4,1)S(1)}, s32[]{:S(2)}) async-start(s8[6291456]{0:T(1024)(128)(4,1)} %bitcast.62), calls=%async_computation.6 | async-start | bytes 8388608
  427.8 9.5 %slice-start.3 = ((s8[6291456]{0:T(1024)(128)(4,1)}), s8[2097152]{0:T(1024)(128)(4,1)S(1)}, s32[]{:S(2)}) async-start(s8[6291456]{0:T(1024)(128)(4,1)} %bitcast.62), calls=%async_computation.7 | async-start | bytes 4194304
Sparse Core Ops, SparseCore 0:
  16.9 135.3 all-reduce.3
  167.6 111.3 all-reduce.5
  442.4 59.3 reduce-scatter.1
where the time goes:
time: 514 us; the launch traced here: 509 us
  waiting for transfers between devices  299 us (58%)
  other arithmetic  125 us (24%)
  matrix products  56.9 us (11%)
  between operations  16.8 us (3%)
  local copies, waits for them, and re-layouts  10.8 us (2%)
    psum x1, waiting for transfers between devices, shards(): sketch = lax.psum(partial_sketch, 'feature') * scale  135 us
    psum x1, waiting for transfers between devices, shards(): gram = lax.psum(local_gram, 'sample')  105 us
    another operation x14, other arithmetic, shards(): lower = jnp.linalg.cholesky(gram)  78.9 us
    reduce_scatter x1, waiting for transfers between devices, shards(): lax.psum_scatter(jnp.dot(basis_t, slab, preferred_element_type=jnp.float3...  58.2 us
    another operation x2, other arithmetic, shards(): lax.linalg.triangular_solve(lower, sketch.T, left_side=True, lower=True)  39.3 us
    another operation x7, matrix products, shards(): lax.linalg.triangular_solve(lower, sketch.T, left_side=True, lower=True)  25.4 us
    dot_general x1, matrix products, shards(): jnp.dot(sketch.T, sketch, preferred_element_type=jnp.float32, precision=l...  15.2 us
  transfers between devices with their start and end apart: 3, of which 3 were waited for; matrix products, arithmetic and copies ran while one was open for 1% of the time, Pallas kernels for 0%

commit v1 on v0

v1 whole, which is shorter than its diff:
```python
import functools
import math

import jax
import jax.numpy as jnp
from jax import lax
from jax.experimental import pallas as pl
from jax.experimental.pallas import tpu as pltpu
from jax.sharding import PartitionSpec as P

D = 16384
F32 = jnp.float32
BF16 = jnp.bfloat16
HIGH = lax.Precision.HIGHEST
MIB = 1 << 20
B = 128
VMEM = pl.BlockSpec(memory_space=pltpu.VMEM)


def remote(src, dst, send_sem, recv_sem, axis, index):
    return pltpu.make_async_remote_copy(
        src_ref=src,
        dst_ref=dst,
        send_sem=send_sem,
        recv_sem=recv_sem,
        device_id={axis: index},
        device_id_type=pl.DeviceIdType.MESH,
    )


def greet(barrier, axis, index):
    pl.semaphore_signal(barrier, inc=1, device_id={axis: index}, device_id_type=pl.DeviceIdType.MESH)


def sketch_kernel(scale, slab_ref, omega_ref, y_ref, wide, tx1, rx1, side1, own1, tx2, rx2, sum2, send_sem, recv_sem):
    f = lax.axis_index("feature")
    x, y = lax.rem(f, 4), f // 4

    def node(axis, pos):
        return 4 * y + pos if axis == 0 else 4 * pos + x

    here = (x, y)
    barrier = pltpu.get_barrier_semaphore()
    for axis in range(2):
        for step in (1, 3):
            greet(barrier, "feature", node(axis, lax.rem(here[axis] + step, 4)))

    wide[...] = omega_ref[...].astype(BF16)
    part = y_ref.shape[1]
    big = 4 * part
    cut = big // 2
    small = part // 2

    def rows(half, pos):
        start = half * 16 * part
        if half == 0:
            blocks = [start + (4 * j + pos) * part for j in range(4)]
            return jnp.concatenate([slab_ref[pl.ds(pl.multiple_of(b, 16), part), :] for b in blocks], axis=0)
        return slab_ref[pl.ds(pl.multiple_of(start + pos * big, 16), big), :]

    def product(half, pos):
        return jnp.dot(rows(half, pos), wide[...], preferred_element_type=F32)

    def send(stage, half, way, piece):
        axis = half if stage == 0 else 1 - half
        to = node(axis, lax.rem(here[axis] + (1 if way == 0 else 3), 4))
        at = ((stage * 2 + half) * 2 + way) * 3 + piece
        tx, rx = (tx1, rx1) if stage == 0 else (tx2, rx2)
        return remote(
            tx.at[half, way, piece], rx.at[half, way, piece], send_sem.at[at], recv_sem.at[at], "feature", to
        )

    copies = []

    def go(*which):
        copy = send(*which)
        copy.start()
        copies.append(copy)

    first = True
    for half in range(2):
        pos = here[half]
        far = product(half, lax.rem(pos + 2, 4)).astype(BF16)
        tx1[half, 0, 0] = far[:cut]
        tx1[half, 1, 0] = far[cut:]
        if first:
            pl.semaphore_wait(barrier, 4)
            first = False
        go(0, half, 0, 0)
        go(0, half, 1, 0)
    for half in range(2):
        pos = here[half]
        right = product(half, lax.rem(pos + 1, 4))
        tx1[half, 0, 1] = right[cut:].astype(BF16)
        go(0, half, 0, 1)
        side1[half, 0] = right[:cut]
        left = product(half, lax.rem(pos + 3, 4))
        tx1[half, 1, 1] = left[:cut].astype(BF16)
        go(0, half, 1, 1)
        side1[half, 1] = left[cut:]
    for half in range(2):
        for way in range(2):
            send(0, half, way, 0).wait_recv()
            tx1[half, way, 2] = (side1[half, way] + rx1[half, way, 0].astype(F32)).astype(BF16)
            go(0, half, way, 2)
    for half in range(2):
        own1[half] = product(half, here[half])
    for half in range(2):
        for way in range(2):
            send(0, half, way, 1).wait_recv()
        own1[half, cut:] += rx1[half, 0, 1].astype(F32)
        own1[half, :cut] += rx1[half, 1, 1].astype(F32)
        for way in range(2):
            send(0, half, way, 2).wait_recv()
        own1[half, :cut] += rx1[half, 0, 2].astype(F32)
        own1[half, cut:] += rx1[half, 1, 2].astype(F32)

        def block(pos, lo, hi):
            return own1[half, pl.ds(pl.multiple_of(pos * part + lo, 8), hi - lo), :]

        pos = here[1 - half]
        far, right, left = (lax.rem(pos + step, 4) for step in (2, 1, 3))
        tx2[half, 0, 0] = block(far, 0, small)
        go(1, half, 0, 0)
        tx2[half, 1, 0] = block(far, small, part)
        go(1, half, 1, 0)
        tx2[half, 0, 1] = block(right, small, part)
        go(1, half, 0, 1)
        tx2[half, 1, 1] = block(left, 0, small)
        go(1, half, 1, 1)
        tx2[half, 0, 2] = block(right, 0, small)
        tx2[half, 1, 2] = block(left, small, part)
        sum2[half] = block(pos, 0, part)
    for half in range(2):
        for way in range(2):
            send(1, half, way, 0).wait_recv()
            tx2[half, way, 2] += rx2[half, way, 0]
            go(1, half, way, 2)
    for half in range(2):
        for way in range(2):
            send(1, half, way, 1).wait_recv()
            send(1, half, way, 2).wait_recv()
        y_ref[half, small:] = (sum2[half, small:] + (rx2[half, 0, 1] + rx2[half, 1, 2])) * scale
        y_ref[half, :small] = (sum2[half, :small] + (rx2[half, 1, 1] + rx2[half, 0, 2])) * scale
    for copy in copies:
        copy.wait_send()


def sketch_part(slab, omega):
    tokens, depth = slab.shape
    k = omega.shape[1]
    part = tokens // 32
    big, cut, small = 4 * part, 2 * part, part // 2
    return pl.pallas_call(
        functools.partial(sketch_kernel, 1.0 / math.sqrt(24.0 * D)),
        out_shape=jax.ShapeDtypeStruct((2, part, k), F32),
        in_specs=[VMEM, VMEM],
        out_specs=VMEM,
        scratch_shapes=[
            pltpu.VMEM((depth, k), BF16),
            pltpu.VMEM((2, 2, 3, cut, k), BF16),
            pltpu.VMEM((2, 2, 3, cut, k), BF16),
            pltpu.VMEM((2, 2, cut, k), F32),
            pltpu.VMEM((2, big, k), F32),
            pltpu.VMEM((2, 2, 3, small, k), F32),
            pltpu.VMEM((2, 2, 3, small, k), F32),
            pltpu.VMEM((2, part, k), F32),
            pltpu.SemaphoreType.DMA((24,)),
            pltpu.SemaphoreType.DMA((24,)),
        ],
        compiler_params=pltpu.CompilerParams(collective_id=0, has_side_effects=True, vmem_limit_bytes=48 * MIB),
        name="sketch",
    )(slab, omega)


def gram_kernel(y_ref, out_ref, packed, rx0, half, rx1, rx2, send_sem, recv_sem):
    f, s = lax.axis_index("feature"), lax.axis_index("sample")
    z, c = s // 2, lax.rem(s, 2)
    twin = 2 * z + 1 - c
    nf = lax.axis_size("feature")
    nz = lax.axis_size("sample") // 2
    barrier = pltpu.get_barrier_semaphore()
    greet(barrier, "sample", twin)
    for d in range(1, nf):
        greet(barrier, "feature", lax.rem(f + d, nf))
    for d in range(1, nz):
        greet(barrier, "sample", lax.rem(s + 2 * d, 2 * nz))

    k = y_ref.shape[2]
    y = y_ref[...].reshape(-1, k)
    yt = y.T
    nb = k // B
    at = 0
    for i in range(nb):
        row = jnp.dot(yt[i * B : (i + 1) * B], y[:, : (i + 1) * B], precision=HIGH, preferred_element_type=F32)
        for j in range(i + 1):
            packed[at * B : (at + 1) * B, :] = row[:, j * B : (j + 1) * B]
            at += 1
    mine = at * B // 2
    part = mine // nf
    pl.semaphore_wait(barrier, nf + nz - 1)

    copies = []

    def go(n, src, dst, axis, index):
        copy = remote(src, dst, send_sem.at[n], recv_sem.at[n], axis, index)
        copy.start()
        copies.append(copy)
        return copy

    base = pl.multiple_of(c * mine, 8)
    other = pl.multiple_of((1 - c) * mine, 8)
    go(0, packed.at[pl.ds(other, mine)], rx0, "sample", twin).wait_recv()
    half[...] = packed[pl.ds(base, mine), :] + rx0[...]

    def share(p):
        return pl.ds(pl.multiple_of(p * part, 8), part)

    got = []
    for d in range(1, nf):
        to = lax.rem(f + d, nf)
        got.append(go(d, half.at[share(to)], rx1.at[d - 1], "feature", to))
    for copy in got:
        copy.wait_recv()
    total = half[share(f), :]
    for d in range(1, nf):
        total += rx1[d - 1]
    rx2[z] = total
    got = []
    for d in range(1, nz):
        to = lax.rem(s + 2 * d, 2 * nz)
        got.append(go(nf + d, rx2.at[z], rx2.at[z], "sample", to))
    for copy in got:
        copy.wait_recv()
    total = rx2[0]
    for d in range(1, nz):
        total += rx2[d]
    own = pl.ds(pl.multiple_of(c * mine + f * part, 8), part)
    out_ref[own, :] = total
    got = []
    for d in range(1, nf):
        got.append(go(nf + nz + d, out_ref.at[own], out_ref.at[own], "feature", lax.rem(f + d, nf)))
    for copy in got:
        copy.wait_recv()
    whole = pl.ds(base, mine)
    go(2 * nf + nz, out_ref.at[whole], out_ref.at[whole], "sample", twin).wait_recv()
    for copy in copies:
        copy.wait_send()


def gram_all(y):
    k = y.shape[2]
    nb = k // B
    rows = nb * (nb + 1) // 2 * B
    nf, nz = lax.axis_size("feature"), lax.axis_size("sample") // 2
    mine = rows // 2
    part = mine // nf
    return pl.pallas_call(
        gram_kernel,
        out_shape=jax.ShapeDtypeStruct((rows, B), F32),
        in_specs=[VMEM],
        out_specs=VMEM,
        scratch_shapes=[
            pltpu.VMEM((rows, B), F32),
            pltpu.VMEM((mine, B), F32),
            pltpu.VMEM((mine, B), F32),
            pltpu.VMEM((nf - 1, part, B), F32),
            pltpu.VMEM((nz, part, B), F32),
            pltpu.SemaphoreType.DMA((2 * nf + nz + 1,)),
            pltpu.SemaphoreType.DMA((2 * nf + nz + 1,)),
        ],
        compiler_params=pltpu.CompilerParams(collective_id=1, has_side_effects=True, vmem_limit_bytes=32 * MIB),
        name="gram",
    )(y)


def rep(x, shape=(8, 128)):
    return jnp.broadcast_to(x, shape)

def chol_block(s, x):
    n = len(s)
    s, x = list(s), list(x)
    ux = []
    for p in range(n):
        k = {}
        for q in range(p + 1, min(n, p + 2)):
            for c in range(8):
                k[q, c] = rep(s[q][:, 8 * p + c : 8 * p + c + 1])
        rg = [rep(s[p][r : r + 1, :]) for r in range(8)]
        rx = [rep(x[p][r : r + 1, :]) for r in range(8)]
        e = {}
        for c in range(8):
            col = rep(s[p][:, 8 * p + c : 8 * p + c + 1])
            for r in range(c, 8):
                e[r, c] = rep(col[r : r + 1, :])
        m = {}
        inv = []
        for r in range(8):
            inv.append(1.0 / e[r, r])
            for t in range(r + 1, 8):
                m[t, r] = e[t, r] * inv[r]
            for t in range(r + 1, 8):
                for c in range(r + 1, t + 1):
                    e[t, c] = e[t, c] - m[t, r] * e[c, r]
            for t in range(r + 1, 8):
                rg[t] = rg[t] - m[t, r] * rg[r]
                rx[t] = rx[t] - m[t, r] * rx[r]
        root = [lax.rsqrt(e[r, r]) for r in range(8)]
        sub = lax.broadcasted_iota(jnp.int32, (8, 128), 0)
        ox = rx[0] * root[0]
        for r in range(1, 8):
            ox = jnp.where(sub == r, rx[r] * root[r], ox)
        ux.append(ox)
        if p + 1 < n:
            wg = [rg[r] * inv[r] for r in range(8)]
            wx = [rx[r] * inv[r] for r in range(8)]
            for r in range(7, -1, -1):
                for t in range(r):
                    wg[t] = wg[t] - m[r, t] * wg[r]
                    wx[t] = wx[t] - m[r, t] * wx[r]
            for q in range(p + 1, n):
                if q > p + 1:
                    for c in range(8):
                        k[q, c] = rep(s[q][:, 8 * p + c : 8 * p + c + 1])
                tg = [k[q, c] * wg[c] for c in range(8)]
                tx = [k[q, c] * wx[c] for c in range(8)]
                s[q] = s[q] - (((tg[0] + tg[1]) + (tg[2] + tg[3])) + ((tg[4] + tg[5]) + (tg[6] + tg[7])))
                x[q] = x[q] - (((tx[0] + tx[1]) + (tx[2] + tx[3])) + ((tx[4] + tx[5]) + (tx[6] + tx[7])))
    return ux

def factor_kernel(tokens, g_ref, lt_ref, inv_ref, w):
    n = w.shape[0]
    at = 0
    for i in range(n // B):
        for j in range(i + 1):
            tile = g_ref[at * B : (at + 1) * B, :]
            w[i * B : (i + 1) * B, j * B : (j + 1) * B] = tile
            if j < i:
                w[j * B : (j + 1) * B, i * B : (i + 1) * B] = tile.T
            at += 1
    scale = 1.0 / math.sqrt(tokens)
    inv_ref[...] = jnp.zeros_like(inv_ref)
    lt_ref[...] = jnp.zeros_like(lt_ref)

    def finish(k, low):
        at, end = k * B, (k + 1) * B
        here = slice(at, end)
        rows = lax.broadcasted_iota(jnp.int32, (B, B), 0)
        cols = lax.broadcasted_iota(jnp.int32, (B, B), 1)
        upper = jnp.dot(low, w[here, here], precision=HIGH, preferred_element_type=F32)
        lt_ref[here, here] = jnp.where(cols >= rows, upper, 0.0) * scale
        inv_ref[here, here] = low
        if at:
            left = jnp.dot(low, w[here, :at], precision=HIGH, preferred_element_type=F32)
            inv_ref[here, :at] = left
        if end < n:
            right = jnp.dot(low, w[here, end:], precision=HIGH, preferred_element_type=F32)
            lt_ref[here, end:] = right * scale
            coef = right.T
            def dot(z):
                return jnp.dot(coef, z, precision=HIGH, preferred_element_type=F32)
            w[end:, end:] -= dot(right)
            w[end:, here] = -dot(low)
            if at:
                w[end:, :at] -= dot(left)

    def step(k, _):
        at = pl.multiple_of(k * B, B)
        here = pl.ds(at, B)
        rid = lax.broadcasted_iota(jnp.int32, (8, B), 0)
        cid = lax.broadcasted_iota(jnp.int32, (8, B), 1)
        s = [w[pl.ds(at + 8 * q, 8), here] for q in range(B // 8)]
        x = [jnp.where(rid + 8 * q == cid, 1.0, 0.0) for q in range(B // 8)]
        ux = chol_block(s, x)
        low = jnp.concatenate(ux, axis=0)
        for j in range(n // B):
            pl.when(k == j)(functools.partial(finish, j, low))
        return 0

    lax.fori_loop(0, n // B, step, 0)


def factor_all(gram, k, tokens):
    return pl.pallas_call(
        functools.partial(factor_kernel, tokens),
        out_shape=(jax.ShapeDtypeStruct((k, k), F32),) * 2,
        in_specs=[VMEM],
        out_specs=[VMEM, VMEM],
        scratch_shapes=[pltpu.VMEM((k, k), F32)],
        compiler_params=pltpu.CompilerParams(vmem_limit_bytes=32 * MIB),
        cost_estimate=pl.CostEstimate(flops=10**10, bytes_accessed=4 * MIB, transcendentals=0),
        name="factor",
    )(gram)


def split(a):
    hi = a.astype(BF16)
    return hi, (a - hi.astype(F32)).astype(BF16)


def project_kernel(inv_ref, z_ref, out_ref, tx0, rx0, own, tx, rx, send_sem, recv_sem):
    s = lax.axis_index("sample")
    nz = lax.axis_size("sample") // 2
    z, c = s // 2, lax.rem(s, 2)
    twin = 2 * z + 1 - c
    ways = [2 * lax.rem(z + 1, nz) + c, 2 * lax.rem(z + nz - 1, nz) + c]
    barrier = pltpu.get_barrier_semaphore()
    for to in (twin, *ways):
        greet(barrier, "sample", to)
    part = out_ref.shape[0]
    cols = out_ref.shape[1] // 2
    cut = part // 2
    hops = nz // 2

    def rows(core):
        picked = [inv_ref[pl.ds(pl.multiple_of((2 * j + core) * part, 8), part), :] for j in range(nz)]
        return split(jnp.concatenate(picked, axis=0))

    def dot(a, b):
        return jnp.dot(a, b, preferred_element_type=F32)

    theirs, ours = rows(1 - c), rows(c)
    copies = []

    def go(n, src, dst, to):
        copy = remote(src, dst, send_sem.at[n], recv_sem.at[n], "sample", to)
        copy.start()
        copies.append(copy)
        return copy

    pair = []
    for h in range(2):
        zh, zl = split(z_ref[:, h * cols : (h + 1) * cols])
        tx0[h] = dot(theirs[0], zh) + (dot(theirs[0], zl) + dot(theirs[1], zh))
        if h == 0:
            pl.semaphore_wait(barrier, 3)
        pair.append(go(h, tx0.at[h], rx0.at[h], twin))
        own[h] = dot(ours[0], zh) + (dot(ours[0], zl) + dot(ours[1], zh))

    def chunk(h, pos, lo=0, hi=part):
        return own[h, pl.ds(pl.multiple_of(pos * part + lo, 8), hi - lo), :]

    ring = {}

    def hop(h, way, j):
        n = 2 + (h * 2 + way) * hops + j
        rows_ = slice(0, cut) if j == 0 else slice(0, part)
        ring[h, way, j] = go(n, tx.at[h, way, j, rows_], rx.at[h, way, j, rows_], ways[way])

    for h in range(2):
        pair[h].wait_recv()
        own[h] += rx0[h]
        far = lax.rem(z + hops, nz)
        tx[h, 0, 0, :cut] = chunk(h, far, 0, cut)
        hop(h, 0, 0)
        tx[h, 1, 0, :cut] = chunk(h, far, cut, part)
        hop(h, 1, 0)
    for j in range(1, hops):
        for h in range(2):
            for way in range(2):
                pos = lax.rem(z + (hops - j if way == 0 else nz - hops + j), nz)
                ring[h, way, j - 1].wait_recv()
                if j == 1:
                    lo, hi = (0, cut) if way == 0 else (cut, part)
                    rest = (cut, part) if way == 0 else (0, cut)
                    tx[h, way, j, lo:hi] = chunk(h, pos, lo, hi) + rx[h, way, 0, :cut]
                    tx[h, way, j, rest[0] : rest[1]] = chunk(h, pos, *rest)
                else:
                    tx[h, way, j] = chunk(h, pos) + rx[h, way, j - 1]
                hop(h, way, j)
    for h in range(2):
        ring[h, 0, hops - 1].wait_recv()
        ring[h, 1, hops - 1].wait_recv()
        out_ref[:, h * cols : (h + 1) * cols] = chunk(h, z) + (rx[h, 0, hops - 1] + rx[h, 1, hops - 1])
    for copy in copies:
        copy.wait_send()


def project_all(inv, zp):
    k, width = zp.shape
    n = lax.axis_size("sample")
    part, cols, hops = k // n, width // 2, n // 4
    ring = (2, 2, hops, part, cols)
    return pl.pallas_call(
        project_kernel,
        out_shape=jax.ShapeDtypeStruct((part, width), F32),
        in_specs=[VMEM, VMEM],
        out_specs=VMEM,
        scratch_shapes=[
            pltpu.VMEM((2, k // 2, cols), F32),
            pltpu.VMEM((2, k // 2, cols), F32),
            pltpu.VMEM((2, k // 2, cols), F32),
            pltpu.VMEM(ring, F32),
            pltpu.VMEM(ring, F32),
            pltpu.SemaphoreType.DMA((2 + 4 * hops,)),
            pltpu.SemaphoreType.DMA((2 + 4 * hops,)),
        ],
        compiler_params=pltpu.CompilerParams(collective_id=2, has_side_effects=True, vmem_limit_bytes=32 * MIB),
        name="project",
    )(inv, zp)


def shards(slab, omega):
    tokens, width = slab.shape
    k = omega.shape[1]
    y = sketch_part(slab, omega)
    halves = [lax.all_gather(y[h].astype(BF16), "feature", axis=0, tiled=True) for h in range(2)]
    lt, inv = factor_all(gram_all(y), k, tokens * lax.axis_size("sample"))
    zp = sum(
        lax.dot_general(
            halves[h],
            slab[h * tokens // 2 : (h + 1) * tokens // 2],
            (((0,), (0,)), ((), ())),
            preferred_element_type=F32,
        )
        for h in range(2)
    )
    return project_all(inv, zp), lt


def solution(mesh):
    placed = (P("sample", "feature"), P("feature", None))
    return jax.shard_map(
        shards, mesh=mesh, in_specs=placed, out_specs=(P("sample", "feature"), P()), check_vma=False
    )
```

time: 514 us -> 179 us (0.35)
  waiting for transfers between devices: 299 us -> 47.4 us
  other arithmetic: 125 us -> 0.03 us
  Pallas kernels: 0 us -> 105 us
  matrix products: 56.9 us -> 8.34 us
  local copies, waits for them, and re-layouts: 10.8 us -> 2.92 us
    psum x2 -> x0, waiting for transfers between devices: 240 us -> none  [the longest x1 135 us: shards(): sketch = lax.psum(partial_sketch, 'feature') * scale]
    another operation x16 -> x1, other arithmetic: 118 us -> 0.03 us  [the longest x14 78.9 us: shards(): lower = jnp.linalg.cholesky(gram)]
    pallas_call x0 -> x4, Pallas kernels: none -> 105 us  [the longest x1 30.4 us: gram_all(): pl.pallas_call(gram_kernel, out_shape=jax.ShapeDtypeStruct((rows, B), F32...]
    reduce_scatter x1 -> x0, waiting for transfers between devices: 58.2 us -> none  [shards(): lax.psum_scatter(jnp.dot(basis_t, slab, preferred_element_type=jnp.float3...]
    all_gather x0 -> x2, waiting for transfers between devices: none -> 46.7 us  [shards(): lax.all_gather(y[h].astype(BF16), 'feature', axis=0, tiled=True)]
    another operation x13 -> x0, matrix products: 27.3 us -> none  [the longest x7 25.4 us: shards(): lax.linalg.triangular_solve(lower, sketch.T, left_side=True, lower=True)]
    dot_general x3 -> x2, matrix products: 29.6 us -> 8.34 us  [shards(): lax.dot_general(halves[h], slab[h * tokens // 2:(h + 1) * tokens // 2], (...]
    another operation x17 -> x0, local copies, waits for them, and re-layouts: 7.77 us -> none
  transfers between devices with their start and end apart: 3 -> 2, of which waited for: 3 -> 1; matrix products, arithmetic and copies ran while one was open for 1% -> 2% of each run, Pallas kernels for 0% -> 30%
where the time goes in v1:
time: 179 us; the launch traced here: 178 us
  Pallas kernels  105 us (59%)
  waiting for transfers between devices  47.4 us (26%)
  between operations  14.1 us (8%)
  matrix products  8.34 us (5%)
  local copies, waits for them, and re-layouts  2.92 us (2%)
    all_gather x2, waiting for transfers between devices, shards(): lax.all_gather(y[h].astype(BF16), 'feature', axis=0, tiled=True)  46.7 us
    pallas_call x1, Pallas kernels, gram_all(): pl.pallas_call(gram_kernel, out_shape=jax.ShapeDtypeStruct((rows, B), F32...  30.4 us
    pallas_call x1, Pallas kernels, sketch_part(): pl.pallas_call(functools.partial(sketch_kernel, 1.0 / math.sqrt(24.0 * D)...  29.8 us
    pallas_call x1, Pallas kernels, factor_all(): pl.pallas_call(functools.partial(factor_kernel, tokens), out_shape=(jax.S...  23.2 us
    pallas_call x1, Pallas kernels, project_all(): pl.pallas_call(project_kernel, out_shape=jax.ShapeDtypeStruct((part, widt...  21.4 us
    dot_general x2, matrix products, shards(): lax.dot_general(halves[h], slab[h * tokens // 2:(h + 1) * tokens // 2], (...  8.34 us
  transfers between devices with their start and end apart: 2, of which 1 were waited for; matrix products, arithmetic and copies ran while one was open for 2% of the time, Pallas kernels for 30%

profile of v1, /device:TPU:2, one launch (start us, length us, event | category | flops | bytes accessed | tf_op | source)
XLA Modules:
  0.0 177.7 jit_solution(5747919914938751014)
XLA Ops:
  7.2 0.0 all-gather.7.cloned.1.call-start
  7.2 0.0 copy-start
  7.2 1.6 copy-done
  8.8 29.8 %sketch.1.y_ref = f32[2,96,512]{2,1,0:T(8,128)S(1)} custom-call(bf16[3072,1024]{1,0:T(8,128)(2,1)} %slab_ref.1, s32[1024,512]{1,0:T(8,128)S(1)} %copy-done), custom_call_target="tpu_custom_call" | custom-call | tf_op jit(solution)/shard_map/sketch/pallas_call | solution.py:154
  38.7 0.7 fusion.11
  39.4 0.0 all-gather.7.cloned.1.call-update
  39.4 0.0 all-gather.5.cloned.1.call-start
  39.4 0.7 all-gather.5.cloned.1.call-update
  40.1 30.4 %gram.1.g_ref = f32[1280,128]{1,0:T(8,128)S(1)} custom-call(f32[2,96,512]{2,1,0:T(8,128)S(1)} %sketch.1.y_ref), custom_call_target="tpu_custom_call" | custom-call | tf_op jit(solution)/shard_map/gram/pallas_call | solution.py:258
  70.5 23.2 %factor.1 = (f32[512,512]{1,0:T(8,128)}, f32[512,512]{1,0:T(8,128)S(1)}) custom-call(f32[1280,128]{1,0:T(8,128)S(1)} %gram.1.g_ref), custom_call_target="tpu_custom_call" | custom-call | flops 10000000000 | bytes 4194304 | tf_op jit(solution)/shard_map/factor/pallas_call | solution.py:384
  93.7 0.0 all-gather.7.cloned.1.call-done
  93.7 4.2 %fusion = f32[512,1024]{1,0:T(8,128)S(1)} fusion(bf16[3072,1024]{1,0:T(8,128)(2,1)} %slab_ref.1, bf16[1,1536,512]{2,1,0:T(8,128)(2,1)} %all-gather.7.cloned.1.call-done), kind=kOutput, calls=%fused_computation | convolution fusion | flops 1610612736 | bytes 6815744 | tf_op jit(solution)/shard_map/dot_general | solution.py:510
  97.9 46.7 %all-gather.5.cloned.1.call-done = bf16[1,1536,512]{2,1,0:T(8,128)(2,1)} async-done(((bf16[1,96,512]{2,1,0:T(8,128)(2,1)}), bf16[1,1536,512]{2,1,0:T(8,128)(2,1)}) %all-gather.5.cloned.1.call-update) | async-done | bytes 1572880 | tf_op jit(solution)/shard_map/all_gather | solution.py:507
  144.5 4.2 %fusion.6.z_ref = f32[512,1024]{1,0:T(8,128)S(1)} fusion(f32[512,1024]{1,0:T(8,128)S(1)} %fusion, bf16[3072,1024]{1,0:T(8,128)(2,1)} %slab_ref.1, bf16[1,1536,512]{2,1,0:T(8,128)(2,1)} %all-gather.5.cloned.1.call-done), kind=kOutput, calls=%fused_computation.6 | convolution fusion | flops 1611137024 | bytes 8912896 | tf_op jit(solution)/shard_map/dot_general | solution.py:510
  148.7 21.4 %project.1 = f32[32,1024]{1,0:T(8,128)S(1)} custom-call(f32[512,512]{1,0:T(8,128)S(1)} %get-tuple-element.4.inv_ref, f32[512,1024]{1,0:T(8,128)S(1)} %fusion.6.z_ref), custom_call_target="tpu_custom_call" | custom-call | tf_op jit(solution)/shard_map/project/pallas_call | solution.py:484
  170.2 0.7 copy.5
  (1 shorter events, 0.0 us)
Async XLA Ops:
  7.2 86.5 %all-gather.7.cloned.1.call-start = ((), (), s32[]{:S(2)}) async-start(), calls=%async_computation.1 | async-start | bytes 1671168 | tf_op jit(solution)/shard_map/all_gather | solution.py:507
  7.2 1.6 copy-start
  39.4 105.2 %all-gather.5.cloned.1.call-start = ((), (), s32[]{:S(2)}) async-start(), calls=%async_computation | async-start | bytes 1671168 | tf_op jit(solution)/shard_map/all_gather | solution.py:507
Sparse Core Ops, SparseCore 0:
  39.5 53.5 all-gather.6
  96.1 48.3 all-gather.4

commit v2 on v0

v2 whole, which is shorter than its diff:
```python
import functools
import math

import jax
import jax.numpy as jnp
from jax import lax
from jax.experimental import pallas as pl
from jax.experimental.pallas import tpu as pltpu
from jax.sharding import PartitionSpec as P

D = 16384
F32 = jnp.float32
BF16 = jnp.bfloat16
HIGH = lax.Precision.HIGHEST
MIB = 1 << 20
B = 128
VMEM = pl.BlockSpec(memory_space=pltpu.VMEM)


def remote(src, dst, send_sem, recv_sem, axis, index):
    return pltpu.make_async_remote_copy(
        src_ref=src,
        dst_ref=dst,
        send_sem=send_sem,
        recv_sem=recv_sem,
        device_id={axis: index},
        device_id_type=pl.DeviceIdType.MESH,
    )


def greet(barrier, axis, index):
    pl.semaphore_signal(barrier, inc=1, device_id={axis: index}, device_id_type=pl.DeviceIdType.MESH)


def rep(a):
    return jnp.broadcast_to(a, a.shape[:-2] + (8, 128))


def inverse_factor(s, hook):
    n = s.shape[0]
    sub = lax.broadcasted_iota(jnp.int32, (8, 128), 0)
    lane = lax.broadcasted_iota(jnp.int32, (8, 128), 1)
    s = [s[q] for q in range(n)]
    x = [jnp.where(sub + 8 * q == lane, 1.0, 0.0) for q in range(n)]
    out = []
    for p in range(n):
        if p == n // 2:
            hook()
        cols = [rep(s[p][:, 8 * p + c : 8 * p + c + 1]) for c in range(8)]
        e = [jnp.stack([rep(cols[c][r : r + 1]) for r in range(c, 8)]) for c in range(8)]
        rg = jnp.stack([rep(s[p][r : r + 1]) for r in range(8)])
        rx = jnp.stack([rep(x[p][r : r + 1]) for r in range(8)])
        m, inv, wg, wx = [], [], [], []
        for r in range(8):
            inv.append(1.0 / e[r][0])
            root = lax.rsqrt(e[r][0])
            o = rx[0] * root
            ox = o if r == 0 else jnp.where(sub == r, o, ox)
            wg.append(rg[0] * inv[r])
            wx.append(rx[0] * inv[r])
            if r == 7:
                break
            m.append(e[r][1:] * inv[r])
            for c in range(r + 1, 8):
                e[c] = e[c] - m[r][c - r - 1 :] * e[r][c - r]
            rg = rg[1:] - m[r] * rg[0]
            rx = rx[1:] - m[r] * rx[0]
        out.append(ox)
        if p + 1 < n:
            for r in range(7, 0, -1):
                for t in range(r):
                    wg[t] = wg[t] - m[t][r - t - 1] * wg[r]
                    wx[t] = wx[t] - m[t][r - t - 1] * wx[r]
            for q in range(p + 1, n):
                k = [rep(s[q][:, 8 * p + c : 8 * p + c + 1]) for c in range(8)]
                for w, v in ((wg, s), (wx, x)):
                    t = [k[c] * w[c] for c in range(8)]
                    v[q] = v[q] - (((t[0] + t[1]) + (t[2] + t[3])) + ((t[4] + t[5]) + (t[6] + t[7])))
    return jnp.concatenate(out, axis=0)


def high(a, b):
    return jnp.dot(a, b, precision=HIGH, preferred_element_type=F32)


def kernel(
    scale, tokens, slab_ref, omega_ref, out_ref, factor_ref,
    wide, tx1, rx1, side1, own1, tx2, rx2, sum2,
    yall, packed, rx0, half_ref, rxp, rxz, gsum,
    zacc, rxt, txr, rxr, zc, cout, w, inv_ref, send_sem, recv_sem,
):
    f, s = lax.axis_index("feature"), lax.axis_index("sample")
    nf, nz = lax.axis_size("feature"), lax.axis_size("sample") // 2
    x, y = lax.rem(f, 4), f // 4
    z, c = s // 2, lax.rem(s, 2)
    twin = 2 * z + 1 - c
    barrier = pltpu.get_barrier_semaphore()
    greet(barrier, "sample", twin)
    for d in range(1, nf):
        greet(barrier, "feature", lax.rem(f + d, nf))
    for d in range(1, nz):
        greet(barrier, "sample", lax.rem(s + 2 * d, 2 * nz))

    copies = []
    count = [0]

    def plan(src, dst, axis, to):
        n = count[0]
        count[0] += 1
        copy = remote(src, dst, send_sem.at[n], recv_sem.at[n], axis, to)
        copies.append(copy)
        return copy

    def go(src, dst, axis, to):
        copy = plan(src, dst, axis, to)
        copy.start()
        return copy

    here = (x, y)

    def node(axis, pos):
        return 4 * y + pos if axis == 0 else 4 * pos + x

    def beside(axis, way):
        return node(axis, lax.rem(here[axis] + (1 if way == 0 else 3), 4))

    wide[...] = omega_ref[...].astype(BF16)
    part = yall.shape[3]
    k = yall.shape[4]
    big = 4 * part
    cut = big // 2
    small = part // 2

    def rows(half, pos):
        start = half * 16 * part
        if half == 0:
            blocks = [start + (4 * j + pos) * part for j in range(4)]
            return jnp.concatenate([slab_ref[pl.ds(pl.multiple_of(b, 16), part), :] for b in blocks], axis=0)
        return slab_ref[pl.ds(pl.multiple_of(start + pos * big, 16), big), :]

    def product(half, pos):
        return jnp.dot(rows(half, pos), wide[...], preferred_element_type=F32)

    sent = {}

    def pass_on(stage, half, way, piece):
        axis = half if stage == 0 else 1 - half
        tx, rx = (tx1, rx1) if stage == 0 else (tx2, rx2)
        sent[stage, half, way, piece] = go(
            tx.at[half, way, piece], rx.at[half, way, piece], "feature", beside(axis, way)
        )

    for half in range(2):
        pos = here[half]
        far = product(half, lax.rem(pos + 2, 4)).astype(BF16)
        tx1[half, 0, 0] = far[:cut]
        tx1[half, 1, 0] = far[cut:]
        if half == 0:
            pl.semaphore_wait(barrier, nf + nz - 1)
        pass_on(0, half, 0, 0)
        pass_on(0, half, 1, 0)
    for half in range(2):
        pos = here[half]
        right = product(half, lax.rem(pos + 1, 4))
        tx1[half, 0, 1] = right[cut:].astype(BF16)
        pass_on(0, half, 0, 1)
        side1[half, 0] = right[:cut]
        left = product(half, lax.rem(pos + 3, 4))
        tx1[half, 1, 1] = left[:cut].astype(BF16)
        pass_on(0, half, 1, 1)
        side1[half, 1] = left[cut:]
    for half in range(2):
        for way in range(2):
            sent[0, half, way, 0].wait_recv()
            tx1[half, way, 2] = (side1[half, way] + rx1[half, way, 0].astype(F32)).astype(BF16)
            pass_on(0, half, way, 2)
    for half in range(2):
        own1[half] = product(half, here[half])
    for half in range(2):
        for way in range(2):
            sent[0, half, way, 1].wait_recv()
        own1[half, cut:] += rx1[half, 0, 1].astype(F32)
        own1[half, :cut] += rx1[half, 1, 1].astype(F32)
        for way in range(2):
            sent[0, half, way, 2].wait_recv()
        own1[half, :cut] += rx1[half, 0, 2].astype(F32)
        own1[half, cut:] += rx1[half, 1, 2].astype(F32)

        def block(pos, lo, hi):
            return own1[half, pl.ds(pl.multiple_of(pos * part + lo, 8), hi - lo), :]

        pos = here[1 - half]
        far, right, left = (lax.rem(pos + step, 4) for step in (2, 1, 3))
        tx2[half, 0, 0] = block(far, 0, small)
        pass_on(1, half, 0, 0)
        tx2[half, 1, 0] = block(far, small, part)
        pass_on(1, half, 1, 0)
        tx2[half, 0, 1] = block(right, small, part)
        pass_on(1, half, 0, 1)
        tx2[half, 1, 1] = block(left, 0, small)
        pass_on(1, half, 1, 1)
        tx2[half, 0, 2] = block(right, 0, small)
        tx2[half, 1, 2] = block(left, small, part)
        sum2[half] = block(pos, 0, part)
    for half in range(2):
        for way in range(2):
            sent[1, half, way, 0].wait_recv()
            tx2[half, way, 2] += rx2[half, way, 0]
            pass_on(1, half, way, 2)
    mine_y = []
    for half in range(2):
        for way in range(2):
            sent[1, half, way, 1].wait_recv()
            sent[1, half, way, 2].wait_recv()
        lower = (sum2[half, small:] + (rx2[half, 0, 1] + rx2[half, 1, 2])) * scale
        upper = (sum2[half, :small] + (rx2[half, 1, 1] + rx2[half, 0, 2])) * scale
        yall[half, y, x] = jnp.concatenate([upper, lower], axis=0).astype(BF16)
        mine_y.append(yall[half, y, x])

    def held(half, stage, px, py, lo=None):
        if stage == 0:
            ref = yall.at[half, py, px]
            return ref if lo is None else ref.at[pl.ds(lo * small, small)]
        if half == 0:
            ref = yall.at[half, py]
            return ref if lo is None else ref.at[pl.ds(2 * lo, 2)]
        return yall.at[half, :, px] if lo is None else yall.at[half, pl.ds(2 * lo, 2), px]

    near, relay = {}, {}

    def spread(stage):
        for half in range(2):
            axis = half if stage == 0 else 1 - half
            for way in range(2):
                ref = held(half, stage, x, y)
                near[stage, half, way] = go(ref, ref, "feature", beside(axis, way))

    def spread_far(stage):
        for half in range(2):
            axis = half if stage == 0 else 1 - half
            for way in range(2):
                near[stage, half, way].wait_recv()
                back = lax.rem(here[axis] + (3 if way == 0 else 1), 4)
                px, py = (back, y) if axis == 0 else (x, back)
                ref = held(half, stage, px, py, way)
                relay[stage, half, way] = go(ref, ref, "feature", beside(axis, way))

    def spread_end(stage):
        for half in range(2):
            for way in range(2):
                relay[stage, half, way].wait_recv()

    spread(0)

    ys = jnp.concatenate(mine_y, axis=0)
    yt = ys.T
    nb = k // B
    at = 0
    for i in range(nb):
        row = jnp.dot(yt[i * B : (i + 1) * B], ys[:, : (i + 1) * B], preferred_element_type=F32)
        for j in range(i + 1):
            packed[at * B : (at + 1) * B, :] = row[:, j * B : (j + 1) * B]
            at += 1
    mine = at * B // 2
    share_rows = mine // nf
    base = pl.multiple_of(c * mine, 8)
    other = pl.multiple_of((1 - c) * mine, 8)
    pair = go(packed.at[pl.ds(other, mine)], rx0, "sample", twin)
    spread_far(0)
    pair.wait_recv()
    half_ref[...] = packed[pl.ds(base, mine), :] + rx0[...]

    def share(p):
        return pl.ds(pl.multiple_of(p * share_rows, 8), share_rows)

    got = []
    for d in range(1, nf):
        to = lax.rem(f + d, nf)
        got.append(go(half_ref.at[share(to)], rxp.at[d - 1], "feature", to))
    spread_end(0)
    spread(1)

    def project(half, py, px, first=False):
        if py is None:
            a = [yall[half, j, px] for j in range(4)]
            t = [half * 16 * part + (4 * j + px) * part for j in range(4)]
            b = [slab_ref[pl.ds(pl.multiple_of(i, 16), part), :] for i in t]
            a, b = jnp.concatenate(a, axis=0), jnp.concatenate(b, axis=0)
        else:
            a = yall[half, py].reshape(big, k)
            b = slab_ref[pl.ds(pl.multiple_of(half * 16 * part + py * big, 16), big), :]
        p = lax.dot_general(a, b, (((0,), (0,)), ((), ())), preferred_element_type=F32)
        zacc[...] = p if first else zacc[...] + p

    project(0, y, None, True)
    project(1, None, x)
    for copy in got:
        copy.wait_recv()
    total = half_ref[share(f), :]
    for d in range(1, nf):
        total += rxp[d - 1]
    rxz[z] = total
    got = []
    for d in range(1, nz):
        got.append(go(rxz.at[z], rxz.at[z], "sample", lax.rem(s + 2 * d, 2 * nz)))
    for copy in got:
        copy.wait_recv()
    total = rxz[0]
    for d in range(1, nz):
        total += rxz[d]
    own = pl.ds(pl.multiple_of(base + f * share_rows, 8), share_rows)
    gsum[own, :] = total
    got = []
    for d in range(1, nf):
        got.append(go(gsum.at[own], gsum.at[own], "feature", lax.rem(f + d, nf)))
    spread_far(1)
    for step in (1, 3):
        project(0, lax.rem(y + step, 4), None)
        project(1, None, lax.rem(x + step, 4))
    for copy in got:
        copy.wait_recv()
    whole = pl.ds(base, mine)
    pair = go(gsum.at[whole], gsum.at[whole], "sample", twin)
    spread_end(1)
    project(0, lax.rem(y + 2, 4), None)
    project(1, None, lax.rem(x + 2, 4))

    keep = k // 2
    theirs = go(zacc.at[pl.ds(pl.multiple_of((1 - c) * keep, 8), keep)], rxt, "sample", twin)
    hops = nz // 2
    ring = {}
    for way in range(2):
        to = 2 * lax.rem(z + (1 if way == 0 else nz - 1), nz) + c
        for j in range(hops):
            part_rows = pl.ds(0, keep // 2 if j == 0 else keep)
            ring[way, j] = plan(txr.at[way, j, part_rows], rxr.at[way, j, part_rows], "sample", to)
    mid = keep // 2

    def chunk(pos, lo=0, hi=keep):
        col = pl.ds(pl.multiple_of(pos * B, B), B)
        return zacc[pl.ds(pl.multiple_of(c * keep + lo, 8), hi - lo), col] + rxt[lo:hi, col]

    def hop(j):
        if j == 0:
            theirs.wait_recv()
        for way in range(2):
            pos = lax.rem(z + (hops - j if way == 0 else nz - hops + j), nz)
            lo = way * mid
            if j == 0:
                txr[way, 0, :mid] = chunk(pos, lo, lo + mid)
            else:
                ring[way, j - 1].wait_recv()
                if j == 1:
                    rest = mid - lo
                    txr[way, 1, lo : lo + mid] = chunk(pos, lo, lo + mid) + rxr[way, 0, :mid]
                    txr[way, 1, rest : rest + mid] = chunk(pos, rest, rest + mid)
                else:
                    txr[way, j] = chunk(pos) + rxr[way, j - 1]
            ring[way, j].start()

    ours = pl.ds(pl.multiple_of(c * keep, 8), keep)
    last = plan(zc.at[ours], zc.at[ours], "sample", twin)

    def meet():
        for way in range(2):
            ring[way, hops - 1].wait_recv()
        zc[ours, :] = chunk(z) + (rxr[0, hops - 1] + rxr[1, hops - 1])
        last.start()

    pair.wait_recv()
    n = k
    at = 0
    for i in range(nb):
        for j in range(i + 1):
            tile = gsum[at * B : (at + 1) * B, :]
            w[i * B : (i + 1) * B, j * B : (j + 1) * B] = tile
            if j < i:
                w[j * B : (j + 1) * B, i * B : (i + 1) * B] = tile.T
            at += 1
    out_scale = 1.0 / math.sqrt(tokens)
    inv_ref[...] = jnp.zeros_like(inv_ref)
    factor_ref[...] = jnp.zeros_like(factor_ref)

    def finish(i, low):
        at, end = i * B, (i + 1) * B
        span = slice(at, end)
        rid = lax.broadcasted_iota(jnp.int32, (B, B), 0)
        cid = lax.broadcasted_iota(jnp.int32, (B, B), 1)
        factor_ref[span, span] = jnp.where(cid >= rid, high(low, w[span, span]), 0.0) * out_scale
        inv_ref[span, span] = low
        if at:
            left = high(low, w[span, :at])
            inv_ref[span, :at] = left
        if end < n:
            right = high(low, w[span, end:])
            factor_ref[span, end:] = right * out_scale
            coef = right.T
            w[end:, end:] -= high(coef, right)
            w[end:, span] = -high(coef, low)
            if at:
                w[end:, :at] -= high(coef, left)

    slots = {1: lambda: hop(0), 2: lambda: hop(1), 4: lambda: hop(2), 5: lambda: hop(3), 7: meet}

    def step(i, _):
        at = pl.multiple_of(i * B, B)

        def hook(second):
            for j, work in slots.items():
                if j % 2 == second:
                    pl.when(i == j // 2)(work)

        hook(0)
        rows_here = w[pl.ds(at, B), pl.ds(at, B)].reshape(B // 8, 8, B)
        low = inverse_factor(rows_here, lambda: hook(1))
        for j in range(nb):
            pl.when(i == j)(functools.partial(finish, j, low))
        return 0

    lax.fori_loop(0, nb, step, 0)

    last.wait_recv()
    out_rows = out_ref.shape[0]
    picked = [inv_ref[pl.ds(pl.multiple_of((2 * j + c) * out_rows, 8), out_rows), :] for j in range(nz)]
    cout[...] = high(jnp.concatenate(picked, axis=0), zc[...]).reshape(cout.shape)
    col = pl.ds(pl.multiple_of(z * B, B), B)
    out_ref[:, col] = cout[z]
    got = []
    for d in range(1, nz):
        to = lax.rem(z + d, nz)
        got.append(go(cout.at[to], out_ref.at[:, col], "sample", 2 * to + c))
    for copy in got:
        copy.wait_recv()
    for copy in copies:
        copy.wait_send()


def shards(slab, omega):
    tokens, width = slab.shape
    depth, k = omega.shape
    nf, ns = lax.axis_size("feature"), lax.axis_size("sample")
    nz = ns // 2
    part = tokens // (2 * nf)
    big, cut, small = 4 * part, 2 * part, part // 2
    nb = k // B
    packed = nb * (nb + 1) // 2 * B
    mine = packed // 2
    share = mine // nf
    keep = k // 2
    sems = 24 + 16 + 2 * nf + nz + 4 * (nz // 2) + nz + 8
    return pl.pallas_call(
        functools.partial(kernel, 1.0 / math.sqrt(24.0 * D), tokens * ns),
        out_shape=(jax.ShapeDtypeStruct((k // ns, width), F32), jax.ShapeDtypeStruct((k, k), F32)),
        in_specs=[VMEM, VMEM],
        out_specs=[VMEM, VMEM],
        scratch_shapes=[
            pltpu.VMEM((depth, k), BF16),
            pltpu.VMEM((2, 2, 3, cut, k), BF16),
            pltpu.VMEM((2, 2, 3, cut, k), BF16),
            pltpu.VMEM((2, 2, cut, k), F32),
            pltpu.VMEM((2, big, k), F32),
            pltpu.VMEM((2, 2, 3, small, k), F32),
            pltpu.VMEM((2, 2, 3, small, k), F32),
            pltpu.VMEM((2, part, k), F32),
            pltpu.VMEM((2, 4, 4, part, k), BF16),
            pltpu.VMEM((packed, B), F32),
            pltpu.VMEM((mine, B), F32),
            pltpu.VMEM((mine, B), F32),
            pltpu.VMEM((nf - 1, share, B), F32),
            pltpu.VMEM((nz, share, B), F32),
            pltpu.VMEM((packed, B), F32),
            pltpu.VMEM((k, width), F32),
            pltpu.VMEM((keep, width), F32),
            pltpu.VMEM((2, nz // 2, keep, B), F32),
            pltpu.VMEM((2, nz // 2, keep, B), F32),
            pltpu.VMEM((k, B), F32),
            pltpu.VMEM((nz, k // ns, B), F32),
            pltpu.VMEM((k, k), F32),
            pltpu.VMEM((k, k), F32),
            pltpu.SemaphoreType.DMA((sems,)),
            pltpu.SemaphoreType.DMA((sems,)),
        ],
        compiler_params=pltpu.CompilerParams(collective_id=0, has_side_effects=True, vmem_limit_bytes=56 * MIB),
        name="range_finder",
    )(slab, omega)


def solution(mesh):
    placed = (P("sample", "feature"), P("feature", None))
    return jax.shard_map(
        shards, mesh=mesh, in_specs=placed, out_specs=(P("sample", "feature"), P()), check_vma=False
    )
```

time: 514 us -> 106 us (0.21); the launches traced: 509 us -> 106 us
  waiting for transfers between devices: 299 us -> 0 us
  other arithmetic: 125 us -> 0 us
  Pallas kernels: 0 us -> 101 us
  matrix products: 56.9 us -> 0 us
  between operations: 16.8 us -> 0.64 us
  local copies, waits for them, and re-layouts: 10.8 us -> 3.83 us
    psum x2 -> x0, waiting for transfers between devices: 240 us -> none  [the longest x1 135 us: shards(): sketch = lax.psum(partial_sketch, 'feature') * scale]
    another operation x16 -> x0, other arithmetic: 118 us -> none  [the longest x14 78.9 us: shards(): lower = jnp.linalg.cholesky(gram)]
    pallas_call x0 -> x1, Pallas kernels: none -> 101 us  [shards(): pl.pallas_call(functools.partial(kernel, 1.0 / math.sqrt(24.0 * D), token...]
    reduce_scatter x1 -> x0, waiting for transfers between devices: 58.2 us -> none  [shards(): lax.psum_scatter(jnp.dot(basis_t, slab, preferred_element_type=jnp.float3...]
    dot_general x3 -> x0, matrix products: 29.6 us -> none  [the longest x1 15.2 us: shards(): jnp.dot(sketch.T, sketch, preferred_element_type=jnp.float32, precision=l...]
    another operation x13 -> x0, matrix products: 27.3 us -> none  [the longest x7 25.4 us: shards(): lax.linalg.triangular_solve(lower, sketch.T, left_side=True, lower=True)]
    another operation x17 -> x0, local copies, waits for them, and re-layouts: 7.77 us -> none
    transpose x1 -> x0, other arithmetic: 6.23 us -> none  [shards(): local_gram = jnp.dot(sketch.T, sketch, preferred_element_type=jnp.float32...]
  transfers between devices with their start and end apart: 3 -> 0, of which waited for: 3 -> 0; matrix products, arithmetic and copies ran while one was open for 1% -> 0% of each run, Pallas kernels for 0% -> 0%
where the time goes in v2:
time: 106 us
  Pallas kernels  101 us (95%)
  local copies, waits for them, and re-layouts  3.83 us (4%)
    pallas_call x1, Pallas kernels, shards(): pl.pallas_call(functools.partial(kernel, 1.0 / math.sqrt(24.0 * D), token...  101 us
    unnamed x2, local copies, waits for them, and re-layouts  3.83 us

profile of v2, /device:TPU:2, one launch (start us, length us, event | category | flops | bytes accessed | tf_op | source)
XLA Modules:
  0.0 105.9 jit_solution(14891891427444751008)
XLA Ops:
  0.6 101.4 %range_finder.1 = (f32[32,1024]{1,0:T(8,128)}, f32[512,512]{1,0:T(8,128)}) custom-call(bf16[3072,1024]{1,0:T(8,128)(2,1)} %slab_ref.1, s32[1024,512]{1,0:T(8,128)} %omega_ref.1), custom_call_target="tpu_custom_call" | custom-call | tf_op jit(solution)/shard_map/range_finder/pallas_call | solution.py:451
  102.0 1.6 %copy.6 = f32[32,1024]{1,0:T(8,128)} copy(f32[32,1024]{1,0:T(8,128)} %get-tuple-element.4) | data formatting | bytes 262144
  103.6 2.3 %copy.7 = f32[512,512]{1,0:T(8,128)} copy(f32[512,512]{1,0:T(8,128)} %get-tuple-element.5) | data formatting | bytes 2097152

commit v3 on v2

--- a/solution.py
+++ b/solution.py
@@ -15,6 +15,7 @@
 MIB = 1 << 20
 B = 128
 VMEM = pl.BlockSpec(memory_space=pltpu.VMEM)
+HBM = pl.BlockSpec(memory_space=pl.ANY)
 
 
 def remote(src, dst, send_sem, recv_sem, axis, index):
@@ -36,7 +37,7 @@
     return jnp.broadcast_to(a, a.shape[:-2] + (8, 128))
 
 
-def inverse_factor(s, hook):
+def inverse_factor(s, rows, hook):
     n = s.shape[0]
     sub = lax.broadcasted_iota(jnp.int32, (8, 128), 0)
     lane = lax.broadcasted_iota(jnp.int32, (8, 128), 1)
@@ -44,33 +45,43 @@
     x = [jnp.where(sub + 8 * q == lane, 1.0, 0.0) for q in range(n)]
     out = []
     for p in range(n):
-        if p == n // 2:
-            hook()
+        if p and p % (n // 4) == 0:
+            hook(p // (n // 4))
         cols = [rep(s[p][:, 8 * p + c : 8 * p + c + 1]) for c in range(8)]
-        e = [jnp.stack([rep(cols[c][r : r + 1]) for r in range(c, 8)]) for c in range(8)]
-        rg = jnp.stack([rep(s[p][r : r + 1]) for r in range(8)])
-        rx = jnp.stack([rep(x[p][r : r + 1]) for r in range(8)])
-        m, inv, wg, wx = [], [], [], []
-        for r in range(8):
-            inv.append(1.0 / e[r][0])
-            root = lax.rsqrt(e[r][0])
-            o = rx[0] * root
-            ox = o if r == 0 else jnp.where(sub == r, o, ox)
-            wg.append(rg[0] * inv[r])
-            wx.append(rx[0] * inv[r])
-            if r == 7:
-                break
-            m.append(e[r][1:] * inv[r])
-            for c in range(r + 1, 8):
-                e[c] = e[c] - m[r][c - r - 1 :] * e[r][c - r]
-            rg = rg[1:] - m[r] * rg[0]
-            rx = rx[1:] - m[r] * rx[0]
+        for c in range(8):
+            rows[c] = cols[c]
+        rows[8] = s[p]
+        rows[9] = x[p]
+        e = {(r, c): rep(rows[c, r : r + 1]) for c in range(8) for r in range(c, 8)}
+        rg = [rep(rows[8, r : r + 1]) for r in range(8)]
+        rx = [rep(rows[9, r : r + 1]) for r in range(8)]
+        m, wg, wx = {}, [None] * 8, [None] * 8
+        for r in range(0, 8, 2):
+            a, b, d = e[r, r], e[r + 1, r], e[r + 1, r + 1]
+            idet = 1.0 / (a * d - b * b)
+            ia = 1.0 / a
+            for t in range(r + 2, 8):
+                m[t, r] = (e[t, r] * d - e[t, r + 1] * b) * idet
+                m[t, r + 1] = (e[t, r + 1] * a - e[t, r] * b) * idet
+            for t in range(r + 2, 8):
+                for c in range(r + 2, t + 1):
+                    e[t, c] = e[t, c] - (m[t, r] * e[c, r] + m[t, r + 1] * e[c, r + 1])
+            for t in range(r + 2, 8):
+                rg[t] = rg[t] - (m[t, r] * rg[r] + m[t, r + 1] * rg[r + 1])
+                rx[t] = rx[t] - (m[t, r] * rx[r] + m[t, r + 1] * rx[r + 1])
+            for v, w in ((rg, wg), (rx, wx)):
+                w[r] = (v[r] * d - v[r + 1] * b) * idet
+                w[r + 1] = (v[r + 1] * a - v[r] * b) * idet
+            o0 = rx[r] * lax.rsqrt(a)
+            o1 = (rx[r + 1] - (b * ia) * rx[r]) * lax.rsqrt((a * d - b * b) * ia)
+            ox = o0 if r == 0 else jnp.where(sub == r, o0, ox)
+            ox = jnp.where(sub == r + 1, o1, ox)
         out.append(ox)
         if p + 1 < n:
-            for r in range(7, 0, -1):
+            for r in range(6, 0, -2):
                 for t in range(r):
-                    wg[t] = wg[t] - m[t][r - t - 1] * wg[r]
-                    wx[t] = wx[t] - m[t][r - t - 1] * wx[r]
+                    wg[t] = wg[t] - (m[r, t] * wg[r] + m[r + 1, t] * wg[r + 1])
+                    wx[t] = wx[t] - (m[r, t] * wx[r] + m[r + 1, t] * wx[r + 1])
             for q in range(p + 1, n):
                 k = [rep(s[q][:, 8 * p + c : 8 * p + c + 1]) for c in range(8)]
                 for w, v in ((wg, s), (wx, x)):
@@ -84,10 +95,10 @@
 
 
 def kernel(
-    scale, tokens, slab_ref, omega_ref, out_ref, factor_ref,
-    wide, tx1, rx1, side1, own1, tx2, rx2, sum2,
+    scale, tokens, slab_hbm, omega_hbm, out_ref, factor_hbm,
+    slab_ref, omega_ref, factor_ref, load_sem, wide, tx1, rx1, side1, own1, tx2, rx2, sum2,
     yall, packed, rx0, half_ref, rxp, rxz, gsum,
-    zacc, rxt, txr, rxr, zc, cout, w, inv_ref, send_sem, recv_sem,
+    zacc, rxt, txr, rxr, zc, cout, w, row_ref, inv_ref, send_sem, recv_sem,
 ):
     f, s = lax.axis_index("feature"), lax.axis_index("sample")
     nf, nz = lax.axis_size("feature"), lax.axis_size("sample") // 2
@@ -101,6 +112,22 @@
     for d in range(1, nz):
         greet(barrier, "sample", lax.rem(s + 2 * d, 2 * nz))
 
+    loads = {}
+    here = (lax.rem(f, 4), f // 4)
+
+    def load(n, src, dst):
+        loads[n] = pltpu.make_async_copy(src, dst, load_sem.at[len(loads)])
+        loads[n].start()
+
+    def tokens_of(ref, half, pos):
+        return ref.at[half, :, pos] if half == 0 else ref.at[half, pos]
+
+    load("omega", omega_hbm, omega_ref)
+    for step in (2, 1, 3, 0):
+        for half in range(2):
+            pos = lax.rem(here[half] + step, 4)
+            load((half, step), tokens_of(slab_hbm, half, pos), tokens_of(slab_ref, half, pos))
+
     copies = []
     count = [0]
 
@@ -116,14 +143,13 @@
         copy.start()
         return copy
 
-    here = (x, y)
-
     def node(axis, pos):
         return 4 * y + pos if axis == 0 else 4 * pos + x
 
     def beside(axis, way):
         return node(axis, lax.rem(here[axis] + (1 if way == 0 else 3), 4))
 
+    loads["omega"].wait()
     wide[...] = omega_ref[...].astype(BF16)
     part = yall.shape[3]
     k = yall.shape[4]
@@ -131,15 +157,10 @@
     cut = big // 2
     small = part // 2
 
-    def rows(half, pos):
-        start = half * 16 * part
-        if half == 0:
-            blocks = [start + (4 * j + pos) * part for j in range(4)]
-            return jnp.concatenate([slab_ref[pl.ds(pl.multiple_of(b, 16), part), :] for b in blocks], axis=0)
-        return slab_ref[pl.ds(pl.multiple_of(start + pos * big, 16), big), :]
-
-    def product(half, pos):
-        return jnp.dot(rows(half, pos), wide[...], preferred_element_type=F32)
+    def product(half, step):
+        loads[half, step].wait()
+        a = tokens_of(slab_ref, half, lax.rem(here[half] + step, 4))[...].reshape(big, -1)
+        return jnp.dot(a, wide[...], preferred_element_type=F32)
 
     sent = {}
 
@@ -151,8 +172,7 @@
         )
 
     for half in range(2):
-        pos = here[half]
-        far = product(half, lax.rem(pos + 2, 4)).astype(BF16)
+        far = product(half, 2).astype(BF16)
         tx1[half, 0, 0] = far[:cut]
         tx1[half, 1, 0] = far[cut:]
         if half == 0:
@@ -160,12 +180,11 @@
         pass_on(0, half, 0, 0)
         pass_on(0, half, 1, 0)
     for half in range(2):
-        pos = here[half]
-        right = product(half, lax.rem(pos + 1, 4))
+        right = product(half, 1)
         tx1[half, 0, 1] = right[cut:].astype(BF16)
         pass_on(0, half, 0, 1)
         side1[half, 0] = right[:cut]
-        left = product(half, lax.rem(pos + 3, 4))
+        left = product(half, 3)
         tx1[half, 1, 1] = left[:cut].astype(BF16)
         pass_on(0, half, 1, 1)
         side1[half, 1] = left[cut:]
@@ -175,7 +194,7 @@
             tx1[half, way, 2] = (side1[half, way] + rx1[half, way, 0].astype(F32)).astype(BF16)
             pass_on(0, half, way, 2)
     for half in range(2):
-        own1[half] = product(half, here[half])
+        own1[half] = product(half, 0)
     for half in range(2):
         for way in range(2):
             sent[0, half, way, 1].wait_recv()
@@ -280,20 +299,17 @@
     spread_end(0)
     spread(1)
 
-    def project(half, py, px, first=False):
-        if py is None:
-            a = [yall[half, j, px] for j in range(4)]
-            t = [half * 16 * part + (4 * j + px) * part for j in range(4)]
-            b = [slab_ref[pl.ds(pl.multiple_of(i, 16), part), :] for i in t]
-            a, b = jnp.concatenate(a, axis=0), jnp.concatenate(b, axis=0)
-        else:
-            a = yall[half, py].reshape(big, k)
-            b = slab_ref[pl.ds(pl.multiple_of(half * 16 * part + py * big, 16), big), :]
+    def project(*steps):
+        a, b = [], []
+        for step in steps:
+            row, col = lax.rem(y + step, 4), lax.rem(x + step, 4)
+            a += [yall[0, row].reshape(big, k), yall[1, :, col].reshape(big, k)]
+            b += [slab_ref[0, row].reshape(big, -1), slab_ref[1, :, col].reshape(big, -1)]
+        a, b = jnp.concatenate(a, axis=0), jnp.concatenate(b, axis=0)
         p = lax.dot_general(a, b, (((0,), (0,)), ((), ())), preferred_element_type=F32)
-        zacc[...] = p if first else zacc[...] + p
-
-    project(0, y, None, True)
-    project(1, None, x)
+        zacc[...] = p if steps == (0,) else zacc[...] + p
+
+    project(0)
     for copy in got:
         copy.wait_recv()
     total = half_ref[share(f), :]
@@ -314,20 +330,32 @@
     for d in range(1, nf):
         got.append(go(gsum.at[own], gsum.at[own], "feature", lax.rem(f + d, nf)))
     spread_far(1)
-    for step in (1, 3):
-        project(0, lax.rem(y + step, 4), None)
-        project(1, None, lax.rem(x + step, 4))
+    project(1, 3)
     for copy in got:
         copy.wait_recv()
     whole = pl.ds(base, mine)
     pair = go(gsum.at[whole], gsum.at[whole], "sample", twin)
-    spread_end(1)
-    project(0, lax.rem(y + 2, 4), None)
-    project(1, None, lax.rem(x + 2, 4))
 
     keep = k // 2
-    theirs = go(zacc.at[pl.ds(pl.multiple_of((1 - c) * keep, 8), keep)], rxt, "sample", twin)
     hops = nz // 2
+
+    def columns(pos):
+        return pl.ds(pl.multiple_of(pos * B, B), B)
+
+    order = sorted(range(nz), key=lambda d: -min(d, nz - d))
+    theirs = {}
+    for d in order:
+        col = columns(lax.rem(z + d, nz))
+        theirs[d] = plan(
+            zacc.at[pl.ds(pl.multiple_of((1 - c) * keep, 8), keep), col], rxt.at[:, col], "sample", twin
+        )
+
+    def finish_product():
+        spread_end(1)
+        project(2)
+        for d in order:
+            theirs[d].start()
+
     ring = {}
     for way in range(2):
         to = 2 * lax.rem(z + (1 if way == 0 else nz - 1), nz) + c
@@ -337,14 +365,15 @@
     mid = keep // 2
 
     def chunk(pos, lo=0, hi=keep):
-        col = pl.ds(pl.multiple_of(pos * B, B), B)
+        col = columns(pos)
         return zacc[pl.ds(pl.multiple_of(c * keep + lo, 8), hi - lo), col] + rxt[lo:hi, col]
 
     def hop(j):
-        if j == 0:
-            theirs.wait_recv()
-        for way in range(2):
-            pos = lax.rem(z + (hops - j if way == 0 else nz - hops + j), nz)
+        for way in range(2):
+            d = hops - j if way == 0 else nz - hops + j
+            pos = lax.rem(z + d, nz)
+            if j or way == 0:
+                theirs[d].wait_recv()
             lo = way * mid
             if j == 0:
                 txr[way, 0, :mid] = chunk(pos, lo, lo + mid)
@@ -362,6 +391,7 @@
     last = plan(zc.at[ours], zc.at[ours], "sample", twin)
 
     def meet():
+        theirs[0].wait_recv()
         for way in range(2):
             ring[way, hops - 1].wait_recv()
         zc[ours, :] = chunk(z) + (rxr[0, hops - 1] + rxr[1, hops - 1])
@@ -369,23 +399,29 @@
 
     pair.wait_recv()
     n = k
+    rid = lax.broadcasted_iota(jnp.int32, (B, B), 0)
+    cid = lax.broadcasted_iota(jnp.int32, (B, B), 1)
+    top = jnp.zeros((B, B), F32)
+    for i in range(nb):
+        last_of_row = (i + 1) * (i + 2) // 2 * B
+        top = jnp.maximum(top, gsum[last_of_row - B : last_of_row, :])
+    top = jnp.max(jnp.where(rid == cid, top, 0.0), axis=(0, 1), keepdims=True)
+    unit = lax.rsqrt(top)
     at = 0
     for i in range(nb):
         for j in range(i + 1):
-            tile = gsum[at * B : (at + 1) * B, :]
+            tile = gsum[at * B : (at + 1) * B, :] * (unit * unit)
             w[i * B : (i + 1) * B, j * B : (j + 1) * B] = tile
             if j < i:
                 w[j * B : (j + 1) * B, i * B : (i + 1) * B] = tile.T
             at += 1
-    out_scale = 1.0 / math.sqrt(tokens)
+    out_scale = (1.0 / math.sqrt(tokens)) / unit
     inv_ref[...] = jnp.zeros_like(inv_ref)
     factor_ref[...] = jnp.zeros_like(factor_ref)
 
     def finish(i, low):
         at, end = i * B, (i + 1) * B
         span = slice(at, end)
-        rid = lax.broadcasted_iota(jnp.int32, (B, B), 0)
-        cid = lax.broadcasted_iota(jnp.int32, (B, B), 1)
         factor_ref[span, span] = jnp.where(cid >= rid, high(low, w[span, span]), 0.0) * out_scale
         inv_ref[span, span] = low
         if at:
@@ -400,30 +436,40 @@
             if at:
                 w[end:, :at] -= high(coef, left)
 
-    slots = {1: lambda: hop(0), 2: lambda: hop(1), 4: lambda: hop(2), 5: lambda: hop(3), 7: meet}
+    slots = {
+        1: finish_product,
+        2: lambda: hop(0),
+        4: lambda: hop(1),
+        7: lambda: hop(2),
+        10: lambda: hop(3),
+        13: meet,
+    }
 
     def step(i, _):
         at = pl.multiple_of(i * B, B)
 
-        def hook(second):
+        def hook(quarter):
             for j, work in slots.items():
-                if j % 2 == second:
-                    pl.when(i == j // 2)(work)
+                if j % 4 == quarter:
+                    pl.when(i == j // 4)(work)
 
         hook(0)
         rows_here = w[pl.ds(at, B), pl.ds(at, B)].reshape(B // 8, 8, B)
-        low = inverse_factor(rows_here, lambda: hook(1))
+        low = inverse_factor(rows_here, row_ref, hook)
         for j in range(nb):
             pl.when(i == j)(functools.partial(finish, j, low))
         return 0
 
     lax.fori_loop(0, nb, step, 0)
 
+    store = pltpu.make_async_copy(factor_ref, factor_hbm, load_sem.at[len(loads)])
+    store.start()
+
     last.wait_recv()
     out_rows = out_ref.shape[0]
     picked = [inv_ref[pl.ds(pl.multiple_of((2 * j + c) * out_rows, 8), out_rows), :] for j in range(nz)]
-    cout[...] = high(jnp.concatenate(picked, axis=0), zc[...]).reshape(cout.shape)
-    col = pl.ds(pl.multiple_of(z * B, B), B)
+    cout[...] = (high(jnp.concatenate(picked, axis=0), zc[...]) * unit).reshape(cout.shape)
+    col = columns(z)
     out_ref[:, col] = cout[z]
     got = []
     for d in range(1, nz):
@@ -433,6 +479,19 @@
         copy.wait_recv()
     for copy in copies:
         copy.wait_send()
+    store.wait()
+
+
+def hand_over(a_ref, b_ref, a_out, b_out, sem):
+    copies = [pltpu.make_async_copy(a_ref, a_out, sem.at[4])]
+    rows = b_ref.shape[0] // 4
+    for j in range(4):
+        part = pl.ds(j * rows, rows)
+        copies.append(pltpu.make_async_copy(b_ref.at[part], b_out.at[part], sem.at[j]))
+    for copy in copies:
+        copy.start()
+    for copy in copies:
+        copy.wait()
 
 
 def shards(slab, omega):
@@ -447,13 +506,17 @@
     mine = packed // 2
     share = mine // nf
     keep = k // 2
-    sems = 24 + 16 + 2 * nf + nz + 4 * (nz // 2) + nz + 8
-    return pl.pallas_call(
+    sems = 24 + 16 + 2 * nf + 2 * nz + 4 * (nz // 2) + nz + 8
+    found = pl.pallas_call(
         functools.partial(kernel, 1.0 / math.sqrt(24.0 * D), tokens * ns),
         out_shape=(jax.ShapeDtypeStruct((k // ns, width), F32), jax.ShapeDtypeStruct((k, k), F32)),
-        in_specs=[VMEM, VMEM],
-        out_specs=[VMEM, VMEM],
+        in_specs=[HBM, HBM],
+        out_specs=[VMEM, HBM],
         scratch_shapes=[
+            pltpu.VMEM((2, 4, 4, part, width), BF16),
+            pltpu.VMEM((depth, k), omega.dtype),
+            pltpu.VMEM((k, k), F32),
+            pltpu.SemaphoreType.DMA((10,)),
             pltpu.VMEM((depth, k), BF16),
             pltpu.VMEM((2, 2, 3, cut, k), BF16),
             pltpu.VMEM((2, 2, 3, cut, k), BF16),
@@ -476,13 +539,23 @@
             pltpu.VMEM((k, B), F32),
             pltpu.VMEM((nz, k // ns, B), F32),
             pltpu.VMEM((k, k), F32),
+            pltpu.VMEM((10, 8, B), F32),
             pltpu.VMEM((k, k), F32),
             pltpu.SemaphoreType.DMA((sems,)),
             pltpu.SemaphoreType.DMA((sems,)),
         ],
         compiler_params=pltpu.CompilerParams(collective_id=0, has_side_effects=True, vmem_limit_bytes=56 * MIB),
         name="range_finder",
-    )(slab, omega)
+    )(slab.reshape(2, 4, 4, part, width), omega)
+    return pl.pallas_call(
+        hand_over,
+        out_shape=tuple(jax.ShapeDtypeStruct(a.shape, a.dtype) for a in found),
+        in_specs=[HBM, HBM],
+        out_specs=[HBM, HBM],
+        scratch_shapes=[pltpu.SemaphoreType.DMA((5,))],
+        compiler_params=pltpu.CompilerParams(vmem_limit_bytes=56 * MIB),
+        name="hand_over",
+    )(*found)
 
 
 def solution(mesh):

time: 106 us -> 132 us (1.25)
  Pallas kernels: 101 us -> 131 us
  local copies, waits for them, and re-layouts: 3.83 us -> 0 us
    pallas_call x0 -> x1, Pallas kernels: none -> 36.9 us  [shards(): pl.pallas_call(hand_over, out_shape=tuple((jax.ShapeDtypeStruct(a.shape,...]
    pallas_call x1, Pallas kernels: 101 us -> 93.9 us  [shards(): pl.pallas_call(functools.partial(kernel, 1.0 / math.sqrt(24.0 * D), token...]
    unnamed x2 -> x0, local copies, waits for them, and re-layouts: 3.83 us -> none
where the time goes in v3:
time: 132 us
  Pallas kernels  131 us (99%)
    pallas_call x1, Pallas kernels, shards(): pl.pallas_call(functools.partial(kernel, 1.0 / math.sqrt(24.0 * D), token...  93.9 us
    pallas_call x1, Pallas kernels, shards(): pl.pallas_call(hand_over, out_shape=tuple((jax.ShapeDtypeStruct(a.shape,...  36.9 us

profile of v3, /device:TPU:2, one launch (start us, length us, event | category | flops | bytes accessed | tf_op | source)
XLA Modules:
  0.0 131.6 jit_solution(5538281489133087355)
XLA Ops:
  0.6 93.9 %range_finder.1 = (f32[32,1024]{1,0:T(8,128)}, f32[512,512]{1,0:T(8,128)}) custom-call(bf16[2,4,4,96,1024]{4,3,2,1,0:T(8,128)(2,1)} %bitcast.1, s32[1024,512]{1,0:T(8,128)} %omega_hbm.1), custom_call_target="tpu_custom_call" | custom-call | tf_op jit(solution)/shard_map/range_finder/pallas_call | solution.py:510
  94.5 36.9 %hand_over.1 = (f32[32,1024]{1,0:T(8,128)}, f32[512,512]{1,0:T(8,128)}) custom-call(f32[32,1024]{1,0:T(8,128)} %get-tuple-element.4.a_ref, f32[512,512]{1,0:T(8,128)} %get-tuple-element.5.b_ref), custom_call_target="tpu_custom_call" | custom-call | tf_op jit(solution)/shard_map/hand_over/pallas_call | solution.py:550

commit v4 on v3

--- a/solution.py
+++ b/solution.py
@@ -97,8 +97,8 @@
 def kernel(
     scale, tokens, slab_hbm, omega_hbm, out_ref, factor_hbm,
     slab_ref, omega_ref, factor_ref, load_sem, wide, tx1, rx1, side1, own1, tx2, rx2, sum2,
-    yall, packed, rx0, half_ref, rxp, rxz, gsum,
-    zacc, rxt, txr, rxr, zc, cout, w, row_ref, inv_ref, send_sem, recv_sem,
+    yall, packed, rx0, half_ref, rxp, line_ref, rxq, rxz, gsum,
+    zacc, rxt, txr, rxr, zc, cout, w, row_ref, inv_ref, send_sem, recv_sem, token_sem,
 ):
     f, s = lax.axis_index("feature"), lax.axis_index("sample")
     nf, nz = lax.axis_size("feature"), lax.axis_size("sample") // 2
@@ -106,11 +106,20 @@
     z, c = s // 2, lax.rem(s, 2)
     twin = 2 * z + 1 - c
     barrier = pltpu.get_barrier_semaphore()
+    up, down = 2 * lax.rem(z + 1, nz) + c, 2 * lax.rem(z + nz - 1, nz) + c
     greet(barrier, "sample", twin)
-    for d in range(1, nf):
-        greet(barrier, "feature", lax.rem(f + d, nf))
-    for d in range(1, nz):
-        greet(barrier, "sample", lax.rem(s + 2 * d, 2 * nz))
+    for d in (1, 3):
+        greet(barrier, "feature", 4 * y + lax.rem(x + d, 4))
+        greet(barrier, "feature", 4 * lax.rem(y + d, 4) + x)
+    for to in (up, down):
+        greet(barrier, "sample", to)
+
+    def token(n):
+        if n:
+            pl.semaphore_wait(token_sem.at[n - 1], 2)
+        if n < nz // 2 - 1:
+            for to in (up, down):
+                greet(token_sem.at[n], "sample", to)
 
     loads = {}
     here = (lax.rem(f, 4), f // 4)
@@ -127,6 +136,7 @@
         for half in range(2):
             pos = lax.rem(here[half] + step, 4)
             load((half, step), tokens_of(slab_hbm, half, pos), tokens_of(slab_ref, half, pos))
+    ready = set()
 
     copies = []
     count = [0]
@@ -154,87 +164,98 @@
     part = yall.shape[3]
     k = yall.shape[4]
     big = 4 * part
-    cut = big // 2
     small = part // 2
-
-    def product(half, step):
-        loads[half, step].wait()
-        a = tokens_of(slab_ref, half, lax.rem(here[half] + step, 4))[...].reshape(big, -1)
-        return jnp.dot(a, wide[...], preferred_element_type=F32)
+    bit = part // 2
+    cut = 2 * bit
+    fine = bit // 2
+    units = [(half, batch) for batch in range(2) for half in range(2)]
+
+    def product(half, batch, step):
+        if (half, step) not in ready:
+            ready.add((half, step))
+            loads[half, step].wait()
+        pos = lax.rem(here[half] + step, 4)
+        lines = pl.ds(batch * bit, bit)
+        a = slab_ref[0, :, pos, lines] if half == 0 else slab_ref[1, pos, :, lines]
+        return jnp.dot(a.reshape(4 * bit, -1), wide[...], preferred_element_type=F32)
 
     sent = {}
 
-    def pass_on(stage, half, way, piece):
+    def pass_on(stage, u, way, piece):
+        half = units[u][0]
         axis = half if stage == 0 else 1 - half
         tx, rx = (tx1, rx1) if stage == 0 else (tx2, rx2)
-        sent[stage, half, way, piece] = go(
-            tx.at[half, way, piece], rx.at[half, way, piece], "feature", beside(axis, way)
-        )
-
-    for half in range(2):
-        far = product(half, 2).astype(BF16)
-        tx1[half, 0, 0] = far[:cut]
-        tx1[half, 1, 0] = far[cut:]
-        if half == 0:
-            pl.semaphore_wait(barrier, nf + nz - 1)
-        pass_on(0, half, 0, 0)
-        pass_on(0, half, 1, 0)
-    for half in range(2):
-        right = product(half, 1)
-        tx1[half, 0, 1] = right[cut:].astype(BF16)
-        pass_on(0, half, 0, 1)
-        side1[half, 0] = right[:cut]
-        left = product(half, 3)
-        tx1[half, 1, 1] = left[:cut].astype(BF16)
-        pass_on(0, half, 1, 1)
-        side1[half, 1] = left[cut:]
-    for half in range(2):
+        sent[stage, u, way, piece] = go(tx.at[u, way, piece], rx.at[u, way, piece], "feature", beside(axis, way))
+
+    for batch in range(2):
+        now = (2 * batch, 2 * batch + 1)
+        for u in now:
+            far = product(*units[u], 2).astype(BF16)
+            tx1[u, 0, 0] = far[:cut]
+            tx1[u, 1, 0] = far[cut:]
+            if u == 0:
+                pl.semaphore_wait(barrier, 7)
+                token(0)
+            pass_on(0, u, 0, 0)
+            pass_on(0, u, 1, 0)
+        for u in now:
+            right = product(*units[u], 1)
+            tx1[u, 0, 1] = right[cut:].astype(BF16)
+            pass_on(0, u, 0, 1)
+            side1[u, 0] = right[:cut]
+            left = product(*units[u], 3)
+            tx1[u, 1, 1] = left[:cut].astype(BF16)
+            pass_on(0, u, 1, 1)
+            side1[u, 1] = left[cut:]
+        for u in now:
+            for way in range(2):
+                sent[0, u, way, 0].wait_recv()
+                tx1[u, way, 2] = (side1[u, way] + rx1[u, way, 0].astype(F32)).astype(BF16)
+                pass_on(0, u, way, 2)
+        token(1 + batch)
+    for u in range(4):
+        own1[u] = product(*units[u], 0)
+    for u in range(4):
+        half = units[u][0]
         for way in range(2):
-            sent[0, half, way, 0].wait_recv()
-            tx1[half, way, 2] = (side1[half, way] + rx1[half, way, 0].astype(F32)).astype(BF16)
-            pass_on(0, half, way, 2)
-    for half in range(2):
-        own1[half] = product(half, 0)
-    for half in range(2):
+            sent[0, u, way, 1].wait_recv()
+        own1[u, cut:] += rx1[u, 0, 1].astype(F32)
+        own1[u, :cut] += rx1[u, 1, 1].astype(F32)
         for way in range(2):
-            sent[0, half, way, 1].wait_recv()
-        own1[half, cut:] += rx1[half, 0, 1].astype(F32)
-        own1[half, :cut] += rx1[half, 1, 1].astype(F32)
-        for way in range(2):
-            sent[0, half, way, 2].wait_recv()
-        own1[half, :cut] += rx1[half, 0, 2].astype(F32)
-        own1[half, cut:] += rx1[half, 1, 2].astype(F32)
+            sent[0, u, way, 2].wait_recv()
+        own1[u, :cut] += rx1[u, 0, 2].astype(F32)
+        own1[u, cut:] += rx1[u, 1, 2].astype(F32)
 
         def block(pos, lo, hi):
-            return own1[half, pl.ds(pl.multiple_of(pos * part + lo, 8), hi - lo), :]
+            return own1[u, pl.ds(pl.multiple_of(pos * bit + lo, 8), hi - lo), :]
 
         pos = here[1 - half]
         far, right, left = (lax.rem(pos + step, 4) for step in (2, 1, 3))
-        tx2[half, 0, 0] = block(far, 0, small)
-        pass_on(1, half, 0, 0)
-        tx2[half, 1, 0] = block(far, small, part)
-        pass_on(1, half, 1, 0)
-        tx2[half, 0, 1] = block(right, small, part)
-        pass_on(1, half, 0, 1)
-        tx2[half, 1, 1] = block(left, 0, small)
-        pass_on(1, half, 1, 1)
-        tx2[half, 0, 2] = block(right, 0, small)
-        tx2[half, 1, 2] = block(left, small, part)
-        sum2[half] = block(pos, 0, part)
-    for half in range(2):
+        tx2[u, 0, 0] = block(far, 0, fine)
+        pass_on(1, u, 0, 0)
+        tx2[u, 1, 0] = block(far, fine, bit)
+        pass_on(1, u, 1, 0)
+        tx2[u, 0, 1] = block(right, fine, bit)
+        pass_on(1, u, 0, 1)
+        tx2[u, 1, 1] = block(left, 0, fine)
+        pass_on(1, u, 1, 1)
+        tx2[u, 0, 2] = block(right, 0, fine)
+        tx2[u, 1, 2] = block(left, fine, bit)
+        sum2[u] = block(pos, 0, bit)
+    for u in range(4):
         for way in range(2):
-            sent[1, half, way, 0].wait_recv()
-            tx2[half, way, 2] += rx2[half, way, 0]
-            pass_on(1, half, way, 2)
-    mine_y = []
-    for half in range(2):
+            sent[1, u, way, 0].wait_recv()
+            tx2[u, way, 2] += rx2[u, way, 0]
+            pass_on(1, u, way, 2)
+    for u in range(4):
+        half, batch = units[u]
         for way in range(2):
-            sent[1, half, way, 1].wait_recv()
-            sent[1, half, way, 2].wait_recv()
-        lower = (sum2[half, small:] + (rx2[half, 0, 1] + rx2[half, 1, 2])) * scale
-        upper = (sum2[half, :small] + (rx2[half, 1, 1] + rx2[half, 0, 2])) * scale
-        yall[half, y, x] = jnp.concatenate([upper, lower], axis=0).astype(BF16)
-        mine_y.append(yall[half, y, x])
+            sent[1, u, way, 1].wait_recv()
+            sent[1, u, way, 2].wait_recv()
+        lower = (sum2[u, fine:] + (rx2[u, 0, 1] + rx2[u, 1, 2])) * scale
+        upper = (sum2[u, :fine] + (rx2[u, 1, 1] + rx2[u, 0, 2])) * scale
+        yall[half, y, x, batch * bit : (batch + 1) * bit] = jnp.concatenate([upper, lower], axis=0).astype(BF16)
+    mine_y = [yall[half, y, x] for half in range(2)]
 
     def held(half, stage, px, py, lo=None):
         if stage == 0:
@@ -289,13 +310,20 @@
     pair.wait_recv()
     half_ref[...] = packed[pl.ds(base, mine), :] + rx0[...]
 
-    def share(p):
-        return pl.ds(pl.multiple_of(p * share_rows, 8), share_rows)
+    line = 4 * share_rows
+    first, second = x + c * (y - x), y + c * (x - y)
+
+    def partner(axis, d):
+        along_y = c if axis == 0 else 1 - c
+        return 4 * lax.rem(y + d * along_y, 4) + lax.rem(x + d * (1 - along_y), 4)
+
+    def span(start, rows):
+        return pl.ds(pl.multiple_of(start, 8), rows)
 
     got = []
-    for d in range(1, nf):
-        to = lax.rem(f + d, nf)
-        got.append(go(half_ref.at[share(to)], rxp.at[d - 1], "feature", to))
+    for d in (2, 1, 3):
+        to = lax.rem(first + d, 4)
+        got.append(go(half_ref.at[span(to * line, line)], rxp.at[d - 1], "feature", partner(0, d)))
     spread_end(0)
     spread(1)
 
@@ -312,10 +340,15 @@
     project(0)
     for copy in got:
         copy.wait_recv()
-    total = half_ref[share(f), :]
-    for d in range(1, nf):
-        total += rxp[d - 1]
-    rxz[z] = total
+    line_ref[...] = half_ref[span(first * line, line), :] + (rxp[0] + rxp[1] + rxp[2])
+    got = []
+    for d in (2, 1, 3):
+        to = lax.rem(second + d, 4)
+        got.append(go(line_ref.at[span(to * share_rows, share_rows)], rxq.at[d - 1], "feature", partner(1, d)))
+    for copy in got:
+        copy.wait_recv()
+    rxz[z] = line_ref[span(second * share_rows, share_rows), :] + (rxq[0] + rxq[1] + rxq[2])
+    token(nz // 2 - 1)
     got = []
     for d in range(1, nz):
         got.append(go(rxz.at[z], rxz.at[z], "sample", lax.rem(s + 2 * d, 2 * nz)))
@@ -324,12 +357,18 @@
     total = rxz[0]
     for d in range(1, nz):
         total += rxz[d]
-    own = pl.ds(pl.multiple_of(base + f * share_rows, 8), share_rows)
+    own = span(base + first * line + second * share_rows, share_rows)
     gsum[own, :] = total
     got = []
-    for d in range(1, nf):
-        got.append(go(gsum.at[own], gsum.at[own], "feature", lax.rem(f + d, nf)))
+    for d in (2, 1, 3):
+        got.append(go(gsum.at[own], gsum.at[own], "feature", partner(1, d)))
     spread_far(1)
+    for copy in got:
+        copy.wait_recv()
+    own = span(base + first * line, line)
+    got = []
+    for d in (2, 1, 3):
+        got.append(go(gsum.at[own], gsum.at[own], "feature", partner(0, d)))
     project(1, 3)
     for copy in got:
         copy.wait_recv()
@@ -396,6 +435,22 @@
             ring[way, hops - 1].wait_recv()
         zc[ours, :] = chunk(z) + (rxr[0, hops - 1] + rxr[1, hops - 1])
         last.start()
+
+    give = []
+    for d in range(1, nz):
+        to = lax.rem(z + d, nz)
+        give.append(plan(cout.at[to], out_ref.at[:, columns(z)], "sample", 2 * to + c))
+
+    def hand_out(lo, hi):
+        if lo == 0:
+            last.wait_recv()
+        part_rows = out_ref.shape[0]
+        picked = [inv_ref[pl.ds(pl.multiple_of((2 * j + c) * part_rows, 8), part_rows), :] for j in range(lo, hi)]
+        p = high(jnp.concatenate(picked, axis=0), zc[...]) * unit
+        cout[lo:hi] = p.reshape(hi - lo, part_rows, B)
+        for d in range(1, nz):
+            to = lax.rem(z + d, nz)
+            pl.when(jnp.logical_and(to >= lo, to < hi))(give[d - 1].start)
 
     pair.wait_recv()
     n = k
@@ -443,6 +498,7 @@
         7: lambda: hop(2),
         10: lambda: hop(3),
         13: meet,
+        15: lambda: hand_out(0, nz - 2),
     }
 
     def step(i, _):
@@ -465,33 +521,30 @@
     store = pltpu.make_async_copy(factor_ref, factor_hbm, load_sem.at[len(loads)])
     store.start()
 
-    last.wait_recv()
-    out_rows = out_ref.shape[0]
-    picked = [inv_ref[pl.ds(pl.multiple_of((2 * j + c) * out_rows, 8), out_rows), :] for j in range(nz)]
-    cout[...] = (high(jnp.concatenate(picked, axis=0), zc[...]) * unit).reshape(cout.shape)
-    col = columns(z)
-    out_ref[:, col] = cout[z]
-    got = []
-    for d in range(1, nz):
-        to = lax.rem(z + d, nz)
-        got.append(go(cout.at[to], out_ref.at[:, col], "sample", 2 * to + c))
-    for copy in got:
+    hand_out(nz - 2, nz)
+    out_ref[:, columns(z)] = cout[z]
+    for copy in give:
         copy.wait_recv()
     for copy in copies:
         copy.wait_send()
     store.wait()
 
 
-def hand_over(a_ref, b_ref, a_out, b_out, sem):
-    copies = [pltpu.make_async_copy(a_ref, a_out, sem.at[4])]
+def hand_over(a_ref, b_ref, a_out, b_out, a_buf, b_buf, sem):
     rows = b_ref.shape[0] // 4
+    jobs = [(a_ref, a_buf, a_out)]
     for j in range(4):
         part = pl.ds(j * rows, rows)
-        copies.append(pltpu.make_async_copy(b_ref.at[part], b_out.at[part], sem.at[j]))
+        jobs.append((b_ref.at[part], b_buf.at[part], b_out.at[part]))
+    copies = [pltpu.make_async_copy(src, buf, sem.at[0, n]) for n, (src, buf, _) in enumerate(jobs)]
     for copy in copies:
         copy.start()
-    for copy in copies:
+    after = [pltpu.make_async_copy(buf, dst, sem.at[1, n]) for n, (_, buf, dst) in enumerate(jobs)]
+    for copy, then in zip(copies, after):
         copy.wait()
+        then.start()
+    for then in after:
+        then.wait()
 
 
 def shards(slab, omega):
@@ -500,13 +553,13 @@
     nf, ns = lax.axis_size("feature"), lax.axis_size("sample")
     nz = ns // 2
     part = tokens // (2 * nf)
-    big, cut, small = 4 * part, 2 * part, part // 2
+    bit = part // 2
     nb = k // B
     packed = nb * (nb + 1) // 2 * B
     mine = packed // 2
     share = mine // nf
     keep = k // 2
-    sems = 24 + 16 + 2 * nf + 2 * nz + 4 * (nz // 2) + nz + 8
+    sems = 48 + 16 + 2 * nf + 2 * nz + 4 * (nz // 2) + nz + 8
     found = pl.pallas_call(
         functools.partial(kernel, 1.0 / math.sqrt(24.0 * D), tokens * ns),
         out_shape=(jax.ShapeDtypeStruct((k // ns, width), F32), jax.ShapeDtypeStruct((k, k), F32)),
@@ -518,18 +571,20 @@
             pltpu.VMEM((k, k), F32),
             pltpu.SemaphoreType.DMA((10,)),
             pltpu.VMEM((depth, k), BF16),
-            pltpu.VMEM((2, 2, 3, cut, k), BF16),
-            pltpu.VMEM((2, 2, 3, cut, k), BF16),
-            pltpu.VMEM((2, 2, cut, k), F32),
-            pltpu.VMEM((2, big, k), F32),
-            pltpu.VMEM((2, 2, 3, small, k), F32),
-            pltpu.VMEM((2, 2, 3, small, k), F32),
-            pltpu.VMEM((2, part, k), F32),
+            pltpu.VMEM((4, 2, 3, part, k), BF16),
+            pltpu.VMEM((4, 2, 3, part, k), BF16),
+            pltpu.VMEM((4, 2, part, k), F32),
+            pltpu.VMEM((4, 2 * part, k), F32),
+            pltpu.VMEM((4, 2, 3, bit // 2, k), F32),
+            pltpu.VMEM((4, 2, 3, bit // 2, k), F32),
+            pltpu.VMEM((4, bit, k), F32),
             pltpu.VMEM((2, 4, 4, part, k), BF16),
             pltpu.VMEM((packed, B), F32),
             pltpu.VMEM((mine, B), F32),
             pltpu.VMEM((mine, B), F32),
-            pltpu.VMEM((nf - 1, share, B), F32),
+            pltpu.VMEM((3, 4 * share, B), F32),
+            pltpu.VMEM((4 * share, B), F32),
+            pltpu.VMEM((3, share, B), F32),
             pltpu.VMEM((nz, share, B), F32),
             pltpu.VMEM((packed, B), F32),
             pltpu.VMEM((k, width), F32),
@@ -543,6 +598,7 @@
             pltpu.VMEM((k, k), F32),
             pltpu.SemaphoreType.DMA((sems,)),
             pltpu.SemaphoreType.DMA((sems,)),
+            pltpu.SemaphoreType.REGULAR((nz // 2 - 1,)),
         ],
         compiler_params=pltpu.CompilerParams(collective_id=0, has_side_effects=True, vmem_limit_bytes=56 * MIB),
         name="range_finder",
@@ -552,7 +608,10 @@
         out_shape=tuple(jax.ShapeDtypeStruct(a.shape, a.dtype) for a in found),
         in_specs=[HBM, HBM],
         out_specs=[HBM, HBM],
-        scratch_shapes=[pltpu.SemaphoreType.DMA((5,))],
+        scratch_shapes=[
+            *(pltpu.VMEM(a.shape, a.dtype) for a in found),
+            pltpu.SemaphoreType.DMA((2, 5)),
+        ],
         compiler_params=pltpu.CompilerParams(vmem_limit_bytes=56 * MIB),
         name="hand_over",
     )(*found)

time: 132 us -> 100 us (0.76)
  Pallas kernels: 131 us -> 98.3 us
    pallas_call x1, Pallas kernels: 36.9 us -> 2.07 us  [shards(): pl.pallas_call(hand_over, out_shape=tuple((jax.ShapeDtypeStruct(a.shape,...]
    pallas_call x1, Pallas kernels: 93.9 us -> 96.2 us  [shards(): pl.pallas_call(functools.partial(kernel, 1.0 / math.sqrt(24.0 * D), token...]
where the time goes in v4:
time: 100 us; the launch traced here: 99.1 us
  Pallas kernels  98.3 us (98%)
    pallas_call x1, Pallas kernels, shards(): pl.pallas_call(functools.partial(kernel, 1.0 / math.sqrt(24.0 * D), token...  96.2 us
    pallas_call x1, Pallas kernels, shards(): pl.pallas_call(hand_over, out_shape=tuple((jax.ShapeDtypeStruct(a.shape,...  2.07 us

profile of v4, /device:TPU:2, one launch (start us, length us, event | category | flops | bytes accessed | tf_op | source)
XLA Modules:
  0.0 99.1 jit_solution(10051637885846502669)
XLA Ops:
  0.6 96.2 %range_finder.1 = (f32[32,1024]{1,0:T(8,128)}, f32[512,512]{1,0:T(8,128)}) custom-call(bf16[2,4,4,96,1024]{4,3,2,1,0:T(8,128)(2,1)} %bitcast.1, s32[1024,512]{1,0:T(8,128)} %omega_hbm.1), custom_call_target="tpu_custom_call" | custom-call | tf_op jit(solution)/shard_map/range_finder/pallas_call | solution.py:563
  96.9 2.1 %hand_over.1 = (f32[32,1024]{1,0:T(8,128)}, f32[512,512]{1,0:T(8,128)}) custom-call(f32[32,1024]{1,0:T(8,128)} %get-tuple-element.4.a_ref, f32[512,512]{1,0:T(8,128)} %get-tuple-element.5.b_ref), custom_call_target="tpu_custom_call" | custom-call | tf_op jit(solution)/shard_map/hand_over/pallas_call | solution.py:606

commit v5 on v4

--- a/solution.py
+++ b/solution.py
@@ -97,8 +97,8 @@
 def kernel(
     scale, tokens, slab_hbm, omega_hbm, out_ref, factor_hbm,
     slab_ref, omega_ref, factor_ref, load_sem, wide, tx1, rx1, side1, own1, tx2, rx2, sum2,
-    yall, packed, rx0, half_ref, rxp, line_ref, rxq, rxz, gsum,
-    zacc, rxt, txr, rxr, zc, cout, w, row_ref, inv_ref, send_sem, recv_sem, token_sem,
+    yall, packed, rx0, half_ref, rxp, rxz, gsum,
+    zacc, rxt, txr, rxr, zc, cout, w, row_ref, inv_ref, send_sem, recv_sem,
 ):
     f, s = lax.axis_index("feature"), lax.axis_index("sample")
     nf, nz = lax.axis_size("feature"), lax.axis_size("sample") // 2
@@ -106,20 +106,11 @@
     z, c = s // 2, lax.rem(s, 2)
     twin = 2 * z + 1 - c
     barrier = pltpu.get_barrier_semaphore()
-    up, down = 2 * lax.rem(z + 1, nz) + c, 2 * lax.rem(z + nz - 1, nz) + c
     greet(barrier, "sample", twin)
-    for d in (1, 3):
-        greet(barrier, "feature", 4 * y + lax.rem(x + d, 4))
-        greet(barrier, "feature", 4 * lax.rem(y + d, 4) + x)
-    for to in (up, down):
-        greet(barrier, "sample", to)
-
-    def token(n):
-        if n:
-            pl.semaphore_wait(token_sem.at[n - 1], 2)
-        if n < nz // 2 - 1:
-            for to in (up, down):
-                greet(token_sem.at[n], "sample", to)
+    for d in range(1, nf):
+        greet(barrier, "feature", lax.rem(f + d, nf))
+    for d in range(1, nz):
+        greet(barrier, "sample", lax.rem(s + 2 * d, 2 * nz))
 
     loads = {}
     here = (lax.rem(f, 4), f // 4)
@@ -194,8 +185,7 @@
             tx1[u, 0, 0] = far[:cut]
             tx1[u, 1, 0] = far[cut:]
             if u == 0:
-                pl.semaphore_wait(barrier, 7)
-                token(0)
+                pl.semaphore_wait(barrier, nf + nz - 1)
             pass_on(0, u, 0, 0)
             pass_on(0, u, 1, 0)
         for u in now:
@@ -212,7 +202,6 @@
                 sent[0, u, way, 0].wait_recv()
                 tx1[u, way, 2] = (side1[u, way] + rx1[u, way, 0].astype(F32)).astype(BF16)
                 pass_on(0, u, way, 2)
-        token(1 + batch)
     for u in range(4):
         own1[u] = product(*units[u], 0)
     for u in range(4):
@@ -310,20 +299,13 @@
     pair.wait_recv()
     half_ref[...] = packed[pl.ds(base, mine), :] + rx0[...]
 
-    line = 4 * share_rows
-    first, second = x + c * (y - x), y + c * (x - y)
-
-    def partner(axis, d):
-        along_y = c if axis == 0 else 1 - c
-        return 4 * lax.rem(y + d * along_y, 4) + lax.rem(x + d * (1 - along_y), 4)
-
-    def span(start, rows):
-        return pl.ds(pl.multiple_of(start, 8), rows)
+    def share(p):
+        return pl.ds(pl.multiple_of(p * share_rows, 8), share_rows)
 
     got = []
-    for d in (2, 1, 3):
-        to = lax.rem(first + d, 4)
-        got.append(go(half_ref.at[span(to * line, line)], rxp.at[d - 1], "feature", partner(0, d)))
+    for d in range(1, nf):
+        to = lax.rem(f + d, nf)
+        got.append(go(half_ref.at[share(to)], rxp.at[d - 1], "feature", to))
     spread_end(0)
     spread(1)
 
@@ -340,15 +322,10 @@
     project(0)
     for copy in got:
         copy.wait_recv()
-    line_ref[...] = half_ref[span(first * line, line), :] + (rxp[0] + rxp[1] + rxp[2])
-    got = []
-    for d in (2, 1, 3):
-        to = lax.rem(second + d, 4)
-        got.append(go(line_ref.at[span(to * share_rows, share_rows)], rxq.at[d - 1], "feature", partner(1, d)))
-    for copy in got:
-        copy.wait_recv()
-    rxz[z] = line_ref[span(second * share_rows, share_rows), :] + (rxq[0] + rxq[1] + rxq[2])
-    token(nz // 2 - 1)
+    total = half_ref[share(f), :]
+    for d in range(1, nf):
+        total += rxp[d - 1]
+    rxz[z] = total
     got = []
     for d in range(1, nz):
         got.append(go(rxz.at[z], rxz.at[z], "sample", lax.rem(s + 2 * d, 2 * nz)))
@@ -357,18 +334,12 @@
     total = rxz[0]
     for d in range(1, nz):
         total += rxz[d]
-    own = span(base + first * line + second * share_rows, share_rows)
+    own = pl.ds(pl.multiple_of(base + f * share_rows, 8), share_rows)
     gsum[own, :] = total
     got = []
-    for d in (2, 1, 3):
-        got.append(go(gsum.at[own], gsum.at[own], "feature", partner(1, d)))
+    for d in range(1, nf):
+        got.append(go(gsum.at[own], gsum.at[own], "feature", lax.rem(f + d, nf)))
     spread_far(1)
-    for copy in got:
-        copy.wait_recv()
-    own = span(base + first * line, line)
-    got = []
-    for d in (2, 1, 3):
-        got.append(go(gsum.at[own], gsum.at[own], "feature", partner(0, d)))
     project(1, 3)
     for copy in got:
         copy.wait_recv()
@@ -582,9 +553,7 @@
             pltpu.VMEM((packed, B), F32),
             pltpu.VMEM((mine, B), F32),
             pltpu.VMEM((mine, B), F32),
-            pltpu.VMEM((3, 4 * share, B), F32),
-            pltpu.VMEM((4 * share, B), F32),
-            pltpu.VMEM((3, share, B), F32),
+            pltpu.VMEM((nf - 1, share, B), F32),
             pltpu.VMEM((nz, share, B), F32),
             pltpu.VMEM((packed, B), F32),
             pltpu.VMEM((k, width), F32),
@@ -598,7 +567,6 @@
             pltpu.VMEM((k, k), F32),
             pltpu.SemaphoreType.DMA((sems,)),
             pltpu.SemaphoreType.DMA((sems,)),
-            pltpu.SemaphoreType.REGULAR((nz // 2 - 1,)),
         ],
         compiler_params=pltpu.CompilerParams(collective_id=0, has_side_effects=True, vmem_limit_bytes=56 * MIB),
         name="range_finder",

time: 100 us -> 94.2 us (0.942)
  Pallas kernels: 98.3 us -> 91.7 us
    pallas_call x1, Pallas kernels: 96.2 us -> 89.6 us  [shards(): pl.pallas_call(functools.partial(kernel, 1.0 / math.sqrt(24.0 * D), token...]
where the time goes in v5:
time: 94.2 us; the launch traced here: 92.5 us
  Pallas kernels  91.7 us (97%)
    pallas_call x1, Pallas kernels, shards(): pl.pallas_call(functools.partial(kernel, 1.0 / math.sqrt(24.0 * D), token...  89.6 us
    pallas_call x1, Pallas kernels, shards(): pl.pallas_call(hand_over, out_shape=tuple((jax.ShapeDtypeStruct(a.shape,...  2.07 us

profile of v5, /device:TPU:2, one launch (start us, length us, event | category | flops | bytes accessed | tf_op | source)
XLA Modules:
  0.0 92.5 jit_solution(7399263404379550989)
XLA Ops:
  0.6 89.6 %range_finder.1 = (f32[32,1024]{1,0:T(8,128)}, f32[512,512]{1,0:T(8,128)}) custom-call(bf16[2,4,4,96,1024]{4,3,2,1,0:T(8,128)(2,1)} %bitcast.1, s32[1024,512]{1,0:T(8,128)} %omega_hbm.1), custom_call_target="tpu_custom_call" | custom-call | tf_op jit(solution)/shard_map/range_finder/pallas_call | solution.py:534
  90.3 2.1 %hand_over.1 = (f32[32,1024]{1,0:T(8,128)}, f32[512,512]{1,0:T(8,128)}) custom-call(f32[32,1024]{1,0:T(8,128)} %get-tuple-element.4.a_ref, f32[512,512]{1,0:T(8,128)} %get-tuple-element.5.b_ref), custom_call_target="tpu_custom_call" | custom-call | tf_op jit(solution)/shard_map/hand_over/pallas_call | solution.py:574

commit v6 on v5

--- a/solution.py
+++ b/solution.py
@@ -122,11 +122,13 @@
     def tokens_of(ref, half, pos):
         return ref.at[half, :, pos] if half == 0 else ref.at[half, pos]
 
-    load("omega", omega_hbm, omega_ref)
-    for step in (2, 1, 3, 0):
+    def load_slab(step):
         for half in range(2):
             pos = lax.rem(here[half] + step, 4)
             load((half, step), tokens_of(slab_hbm, half, pos), tokens_of(slab_ref, half, pos))
+
+    load("omega", omega_hbm, omega_ref)
+    load_slab(2)
     ready = set()
 
     copies = []
@@ -151,6 +153,8 @@
         return node(axis, lax.rem(here[axis] + (1 if way == 0 else 3), 4))
 
     loads["omega"].wait()
+    for step in (1, 3, 0):
+        load_slab(step)
     wide[...] = omega_ref[...].astype(BF16)
     part = yall.shape[3]
     k = yall.shape[4]
@@ -258,21 +262,27 @@
     near, relay = {}, {}
 
     def spread(stage):
-        for half in range(2):
-            axis = half if stage == 0 else 1 - half
-            for way in range(2):
-                ref = held(half, stage, x, y)
-                near[stage, half, way] = go(ref, ref, "feature", beside(axis, way))
+        for lo in range(2):
+            for half in range(2):
+                axis = half if stage == 0 else 1 - half
+                for way in range(2):
+                    ref = held(half, stage, x, y, way if lo == 0 else 1 - way)
+                    near[stage, half, way, lo] = go(ref, ref, "feature", beside(axis, way))
 
     def spread_far(stage):
         for half in range(2):
             axis = half if stage == 0 else 1 - half
             for way in range(2):
-                near[stage, half, way].wait_recv()
+                near[stage, half, way, 0].wait_recv()
                 back = lax.rem(here[axis] + (3 if way == 0 else 1), 4)
                 px, py = (back, y) if axis == 0 else (x, back)
                 ref = held(half, stage, px, py, way)
                 relay[stage, half, way] = go(ref, ref, "feature", beside(axis, way))
+
+    def spread_near(stage):
+        for half in range(2):
+            for way in range(2):
+                near[stage, half, way, 1].wait_recv()
 
     def spread_end(stage):
         for half in range(2):
@@ -306,6 +316,7 @@
     for d in range(1, nf):
         to = lax.rem(f + d, nf)
         got.append(go(half_ref.at[share(to)], rxp.at[d - 1], "feature", to))
+    spread_near(0)
     spread_end(0)
     spread(1)
 
@@ -329,6 +340,7 @@
     got = []
     for d in range(1, nz):
         got.append(go(rxz.at[z], rxz.at[z], "sample", lax.rem(s + 2 * d, 2 * nz)))
+    spread_far(1)
     for copy in got:
         copy.wait_recv()
     total = rxz[0]
@@ -339,12 +351,8 @@
     got = []
     for d in range(1, nf):
         got.append(go(gsum.at[own], gsum.at[own], "feature", lax.rem(f + d, nf)))
-    spread_far(1)
+    spread_near(1)
     project(1, 3)
-    for copy in got:
-        copy.wait_recv()
-    whole = pl.ds(base, mine)
-    pair = go(gsum.at[whole], gsum.at[whole], "sample", twin)
 
     keep = k // 2
     hops = nz // 2
@@ -406,6 +414,13 @@
             ring[way, hops - 1].wait_recv()
         zc[ours, :] = chunk(z) + (rxr[0, hops - 1] + rxr[1, hops - 1])
         last.start()
+
+    finish_product()
+    for copy in got:
+        copy.wait_recv()
+    whole = pl.ds(base, mine)
+    pair = go(gsum.at[whole], gsum.at[whole], "sample", twin)
+    hop(0)
 
     give = []
     for d in range(1, nz):
@@ -463,13 +478,11 @@
                 w[end:, :at] -= high(coef, left)
 
     slots = {
-        1: finish_product,
-        2: lambda: hop(0),
-        4: lambda: hop(1),
-        7: lambda: hop(2),
-        10: lambda: hop(3),
-        13: meet,
-        15: lambda: hand_out(0, nz - 2),
+        0: lambda: hop(1),
+        3: lambda: hop(2),
+        6: lambda: hop(3),
+        10: meet,
+        13: lambda: hand_out(0, nz - 2),
     }
 
     def step(i, _):
@@ -530,7 +543,7 @@
     mine = packed // 2
     share = mine // nf
     keep = k // 2
-    sems = 48 + 16 + 2 * nf + 2 * nz + 4 * (nz // 2) + nz + 8
+    sems = 48 + 24 + 2 * nf + 2 * nz + 4 * (nz // 2) + nz + 8
     found = pl.pallas_call(
         functools.partial(kernel, 1.0 / math.sqrt(24.0 * D), tokens * ns),
         out_shape=(jax.ShapeDtypeStruct((k // ns, width), F32), jax.ShapeDtypeStruct((k, k), F32)),

time: 94.2 us -> 91.7 us (0.973); the launches traced: 92.5 us -> 91.2 us
  Pallas kernels: 91.7 us -> 90.4 us
    pallas_call x1, Pallas kernels: 89.6 us -> 88.4 us  [shards(): pl.pallas_call(functools.partial(kernel, 1.0 / math.sqrt(24.0 * D), token...]
where the time goes in v6:
time: 91.7 us; the launch traced here: 91.2 us
  Pallas kernels  90.4 us (99%)
    pallas_call x1, Pallas kernels, shards(): pl.pallas_call(functools.partial(kernel, 1.0 / math.sqrt(24.0 * D), token...  88.4 us
    pallas_call x1, Pallas kernels, shards(): pl.pallas_call(hand_over, out_shape=tuple((jax.ShapeDtypeStruct(a.shape,...  2.07 us

profile of v6, /device:TPU:2, one launch (start us, length us, event | category | flops | bytes accessed | tf_op | source)
XLA Modules:
  0.0 91.2 jit_solution(17280569174630179395)
XLA Ops:
  0.6 88.4 %range_finder.1 = (f32[32,1024]{1,0:T(8,128)}, f32[512,512]{1,0:T(8,128)}) custom-call(bf16[2,4,4,96,1024]{4,3,2,1,0:T(8,128)(2,1)} %bitcast.1, s32[1024,512]{1,0:T(8,128)} %omega_hbm.1), custom_call_target="tpu_custom_call" | custom-call | tf_op jit(solution)/shard_map/range_finder/pallas_call | solution.py:547
  89.0 2.1 %hand_over.1 = (f32[32,1024]{1,0:T(8,128)}, f32[512,512]{1,0:T(8,128)}) custom-call(f32[32,1024]{1,0:T(8,128)} %get-tuple-element.4.a_ref, f32[512,512]{1,0:T(8,128)} %get-tuple-element.5.b_ref), custom_call_target="tpu_custom_call" | custom-call | tf_op jit(solution)/shard_map/hand_over/pallas_call | solution.py:587

commit v7 on v6

--- a/solution.py
+++ b/solution.py
@@ -98,7 +98,7 @@
     scale, tokens, slab_hbm, omega_hbm, out_ref, factor_hbm,
     slab_ref, omega_ref, factor_ref, load_sem, wide, tx1, rx1, side1, own1, tx2, rx2, sum2,
     yall, packed, rx0, half_ref, rxp, rxz, gsum,
-    zacc, rxt, txr, rxr, zc, cout, w, row_ref, inv_ref, send_sem, recv_sem,
+    zacc, rxt, txr, rxr, zc, cout, w, row_ref, inv_ref, send_sem, recv_sem, token_sem,
 ):
     f, s = lax.axis_index("feature"), lax.axis_index("sample")
     nf, nz = lax.axis_size("feature"), lax.axis_size("sample") // 2
@@ -106,11 +106,20 @@
     z, c = s // 2, lax.rem(s, 2)
     twin = 2 * z + 1 - c
     barrier = pltpu.get_barrier_semaphore()
+    up, down = 2 * lax.rem(z + 1, nz) + c, 2 * lax.rem(z + nz - 1, nz) + c
     greet(barrier, "sample", twin)
-    for d in range(1, nf):
-        greet(barrier, "feature", lax.rem(f + d, nf))
-    for d in range(1, nz):
-        greet(barrier, "sample", lax.rem(s + 2 * d, 2 * nz))
+    for d in (1, 3):
+        greet(barrier, "feature", 4 * y + lax.rem(x + d, 4))
+        greet(barrier, "feature", 4 * lax.rem(y + d, 4) + x)
+    for to in (up, down):
+        greet(barrier, "sample", to)
+
+    def token(n):
+        if n:
+            pl.semaphore_wait(token_sem.at[n - 1], 2)
+        if n < nz // 2 - 1:
+            for to in (up, down):
+                greet(token_sem.at[n], "sample", to)
 
     loads = {}
     here = (lax.rem(f, 4), f // 4)
@@ -189,7 +198,8 @@
             tx1[u, 0, 0] = far[:cut]
             tx1[u, 1, 0] = far[cut:]
             if u == 0:
-                pl.semaphore_wait(barrier, nf + nz - 1)
+                pl.semaphore_wait(barrier, 7)
+                token(0)
             pass_on(0, u, 0, 0)
             pass_on(0, u, 1, 0)
         for u in now:
@@ -206,6 +216,7 @@
                 sent[0, u, way, 0].wait_recv()
                 tx1[u, way, 2] = (side1[u, way] + rx1[u, way, 0].astype(F32)).astype(BF16)
                 pass_on(0, u, way, 2)
+        token(1 + batch)
     for u in range(4):
         own1[u] = product(*units[u], 0)
     for u in range(4):
@@ -337,6 +348,7 @@
     for d in range(1, nf):
         total += rxp[d - 1]
     rxz[z] = total
+    token(nz // 2 - 1)
     got = []
     for d in range(1, nz):
         got.append(go(rxz.at[z], rxz.at[z], "sample", lax.rem(s + 2 * d, 2 * nz)))
@@ -580,6 +592,7 @@
             pltpu.VMEM((k, k), F32),
             pltpu.SemaphoreType.DMA((sems,)),
             pltpu.SemaphoreType.DMA((sems,)),
+            pltpu.SemaphoreType.REGULAR((nz // 2 - 1,)),
         ],
         compiler_params=pltpu.CompilerParams(collective_id=0, has_side_effects=True, vmem_limit_bytes=56 * MIB),
         name="range_finder",

time: 91.7 us -> 91 us (level)
  no operation moved by 1% of the time
where the time goes in v7:
time: 91 us; the launch traced here: 90.5 us
  Pallas kernels  89.7 us (99%)
    pallas_call x1, Pallas kernels, shards(): pl.pallas_call(functools.partial(kernel, 1.0 / math.sqrt(24.0 * D), token...  87.6 us
    pallas_call x1, Pallas kernels, shards(): pl.pallas_call(hand_over, out_shape=tuple((jax.ShapeDtypeStruct(a.shape,...  2.07 us

profile of v7, /device:TPU:2, one launch (start us, length us, event | category | flops | bytes accessed | tf_op | source)
XLA Modules:
  0.0 90.5 jit_solution(4037060609708829423)
XLA Ops:
  0.6 87.6 %range_finder.1 = (f32[32,1024]{1,0:T(8,128)}, f32[512,512]{1,0:T(8,128)}) custom-call(bf16[2,4,4,96,1024]{4,3,2,1,0:T(8,128)(2,1)} %bitcast.1, s32[1024,512]{1,0:T(8,128)} %omega_hbm.1), custom_call_target="tpu_custom_call" | custom-call | tf_op jit(solution)/shard_map/range_finder/pallas_call | solution.py:559
  88.2 2.1 %hand_over.1 = (f32[32,1024]{1,0:T(8,128)}, f32[512,512]{1,0:T(8,128)}) custom-call(f32[32,1024]{1,0:T(8,128)} %get-tuple-element.4.a_ref, f32[512,512]{1,0:T(8,128)} %get-tuple-element.5.b_ref), custom_call_target="tpu_custom_call" | custom-call | tf_op jit(solution)/shard_map/hand_over/pallas_call | solution.py:600
